TPU v7x, 256 devices: a whole 4x4x8 slice. The times are simulated.
256 devices in a mesh: dp: 32 (over y, x, core), tensor: 8 (over z).
Axes of the slice: x: 4, y: 4, z: 8, core: 2. Of those that a mesh axis runs over, the one named last changes fastest.
Arguments:
- inputs: bfloat16 [8192, 4096], P('dp', 'tensor'), may hold values from -6 to 6
- weight: bfloat16 [4096, 4096], P('tensor'), may hold values from -0.046875 to 0.046875
- out_grad: bfloat16 [8192, 4096], P(('dp', 'tensor')), may hold values from -0.25 to 0.25
- error_feedback: bfloat16 [32, 4096, 4096], P('dp', 'tensor'), may hold values from -4 to 4
- warm_coeffs: float32 [8, 8, 4096], P('tensor'), may hold values from -6 to 6
Outputs:
- outputs: bfloat16 [8192, 4096], P(('dp', 'tensor'))
- new_basis: float32 [8, 4096], P(None, 'tensor')
- new_coeffs: float32 [8, 8, 4096], P('tensor')
- new_error: bfloat16 [32, 4096, 4096], P('dp', 'tensor')
All inputs are finite; a program needn't handle non-finite values.
Results may differ from a plain program's by a relative error of at most 0.001.
Values may be sent and summed in bfloat16 or wider, within the bound.
A program may use at most 128 MiB of HBM per device.

v0:
```python
import math

import jax
import jax.numpy as jnp
from jax import lax
from jax.sharding import PartitionSpec as P

exact_precision = lax.Precision.HIGHEST
epsilon = 1e-06


def gram_schmidt(sketch_rows):
    kept_rows = []
    for row_index in range(sketch_rows.shape[0]):
        vector = sketch_rows[row_index]
        for earlier in kept_rows:
            vector = vector - jnp.sum(vector * earlier) * earlier
        vector = vector * lax.rsqrt(jnp.sum(vector * vector) + epsilon)
        kept_rows.append(vector)
    return jnp.stack(kept_rows)


def shards(inputs, weight, out_grad, error_feedback, warm_coeffs):
    shard_rows = inputs.shape[1]
    replica_count = lax.axis_size("dp")
    token_rows = inputs
    outputs = lax.psum_scatter(
        jnp.dot(token_rows, weight, preferred_element_type=jnp.float32),
        "tensor",
        scatter_dimension=0,
        tiled=True,
    ).astype(jnp.bfloat16)
    token_rows = inputs
    gradient = lax.dot_general(
        token_rows,
        lax.all_gather(out_grad, "tensor", axis=0, tiled=True),
        (((0,), (0,)), ((), ())),
        preferred_element_type=jnp.float32,
    )
    merged = error_feedback[0].astype(jnp.float32) + gradient
    sketch = lax.dot_general(
        warm_coeffs[0],
        merged,
        (((1,), (1,)), ((), ())),
        precision=exact_precision,
        preferred_element_type=jnp.float32,
    )
    sketch = lax.psum(sketch, "dp")
    unit_rows = gram_schmidt(sketch)
    coefficients = jnp.dot(
        unit_rows, merged, precision=exact_precision, preferred_element_type=jnp.float32
    )
    coefficients = lax.psum(coefficients, "dp") / replica_count
    approx = lax.dot_general(
        unit_rows,
        coefficients,
        (((0,), (0,)), ((), ())),
        precision=exact_precision,
        preferred_element_type=jnp.float32,
    )
    new_error = (merged - approx).astype(jnp.bfloat16)[None]
    new_basis = unit_rows * math.sqrt(shard_rows)
    return (outputs, new_basis, coefficients[None], new_error)


def solution(mesh):
    in_specs = (
        P("dp", "tensor"),
        P("tensor", None),
        P(("dp", "tensor"), None),
        P("dp", "tensor", None),
        P("tensor", None, None),
    )
    out_specs = (
        P(("dp", "tensor"), None),
        P(None, "tensor"),
        P("tensor", None, None),
        P("dp", "tensor", None),
    )
    return jax.shard_map(shards, mesh=mesh, in_specs=in_specs, out_specs=out_specs, check_vma=False)
```

profile of v0, /device:TPU:1, one launch (start us, length us, event | category | flops | bytes accessed | tf_op | source)
XLA Modules:
  0.0 430.7 jit_solution(12019045929572137182)
XLA Ops:
  7.2 0.0 copy-start
  7.2 0.0 all-gather.2.cloned.1.call-start
  7.2 0.7 all-gather.2.cloned.1.call-update
  7.9 0.0 copy-start.3
  7.9 0.0 all-reduce.2.cloned.1.call-start
  8.0 43.1 %all-gather.2.cloned.1.call-done = bf16[256,4096]{1,0:T(8,128)(2,1)} async-done(((bf16[32,4096]{1,0:T(8,128)(2,1)}), bf16[256,4096]{1,0:T(8,128)(2,1)}) %all-gather.2.cloned.1.call-update) | async-done | bytes 2097168 | tf_op jit(solution)/shard_map/all_gather | solution.py:36
  51.0 0.0 copy-done
  51.0 4.1 convert_add_fusion
  55.2 0.0 copy-start.1
  55.2 3.2 copy-done.1
  58.4 0.0 copy-done.3
  58.4 7.2 %convolution_bitcast_fusion = f32[8,512]{1,0:T(8,128)S(1)} fusion(f32[512,4096]{1,0:T(8,128)S(1)} %convert_add_fusion, f32[1,8,4096]{2,1,0:T(8,128)S(1)} %copy-done.3), kind=kOutput, calls=%fused_computation.3 | convolution fusion | flops 201326592 | bytes 8536064 | tf_op jit(solution)/shard_map/dot_general | solution.py:41
  65.6 123.1 %psum.14 = f32[8,512]{1,0:T(8,128)S(1)} all-reduce(f32[8,512]{1,0:T(8,128)S(1)} %convolution_bitcast_fusion), channel_id=1, replica_groups=mesh['dp'=32,'tensor'=8] {'dp'}, use_global_device_ids=true, to_apply=%region_1.0 | all-reduce | flops 4096 | bytes 32768 | tf_op jit(solution)/shard_map/psum | solution.py:48
  188.6 0.6 multiply_reduce_fusion.35
  189.9 0.6 multiply_reduce_fusion.34
  190.5 1.3 multiply_reduce_fusion.7
  192.5 5.0 %multiply_reduce_fusion.6 = (f32[]{:T(128)}, f32[]{:T(128)}, f32[]{:T(128)}, f32[]{:T(128)}, f32[]{:T(128)}, /*index=5*/f32[]{:T(128)}, f32[512]{0:T(512)S(1)}) fusion(f32[512]{0:T(512)S(1)} %bitcast.35, f32[512]{0:T(512)S(1)} %bitcast.30, f32[]{:T(128)} %get-tuple-element.24, f32[512]{0:T(512)S(1)} %bitcast.38, f32[]{:T(128)} %get-tuple-element.25, ...), kind=kLoop, calls=%fused_computation.21 | loop fusion | flops 13818 | bytes 18488 | tf_op jit(solution)/shard_map/reduce_sum | solution.py:17
  197.5 1.9 multiply_reduce_fusion.30
  200.1 1.9 multiply_reduce_fusion.27
  202.0 6.3 %multiply_reduce_fusion.5 = (f32[]{:T(128)}, f32[]{:T(128)}, f32[]{:T(128)}, f32[]{:T(128)}, f32[]{:T(128)}, /*index=5*/f32[512]{0:T(512)S(1)}, f32[512]{0:T(512)S(1)}, f32[512]{0:T(512)S(1)}, f32[512]{0:T(512)S(1)}) fusion(f32[512]{0:T(512)S(1)} %get-tuple-element.55, f32[512]{0:T(512)S(1)} %get-tuple-element.54, f32[]{:T(128)} %get-tuple-element.53, ...), kind=kLoop, calls=%fused_computation.19 | loop fusion | flops 14331 | bytes 24632 | tf_op jit(solution)/shard_map/reduce_sum | solution.py:17
  208.9 3.8 multiply_reduce_fusion.4
  212.8 1.9 multiply_reduce_fusion.21
  215.3 1.8 multiply_reduce_fusion.16
  217.1 3.8 multiply_reduce_fusion.3
  221.5 2.5 multiply_reduce_fusion.2
  224.0 2.5 multiply_reduce_fusion.8
  227.1 2.4 multiply_reduce_fusion.1
  229.5 1.2 multiply_reduce_fusion
  231.4 17.4 %subtract_multiply_fusion = (f32[1,512]{1,0:T(1,128)S(1)}, f32[1,512]{1,0:T(1,128)S(1)}, f32[1,512]{1,0:T(1,128)S(1)}, f32[1,512]{1,0:T(1,128)S(1)}, f32[1,512]{...) fusion(f32[1,512]{1,0:T(1,128)S(1)} %get-tuple-element.60, f32[]{:T(128)S(6)} %rsqrt.31, ...), kind=kLoop, calls=%fused_computation.10 | loop fusion | flops 32256 | bytes 30860 | tf_op jit(solution)/shard_map/mul | solution.py:18
  248.8 7.0 %fusion.7 = f32[8,4096]{1,0:T(8,128)} fusion(f32[8,512]{1,0:T(8,128)S(1)} %stack.2, f32[512,4096]{1,0:T(8,128)} %copy-done.1), kind=kOutput, calls=%fused_computation.87 | convolution fusion | flops 201326592 | bytes 8536064 | tf_op jit(solution)/shard_map/dot_general | solution.py:50
  255.8 0.0 all-reduce.2.cloned.1.call-update
  255.8 0.2 reduce-scatter.2.cloned.1.call-start
  256.0 5.4 %fusion.6 = f32[256,4096]{1,0:T(8,128)} fusion(bf16[256,512]{1,0:T(8,128)(2,1)S(1)} %copy-done, bf16[512,4096]{1,0:T(8,128)(2,1)} %param.6), kind=kOutput, calls=%fused_computation.86 | convolution fusion | flops 1073741824 | bytes 8650752 | tf_op jit(solution)/shard_map/dot_general | solution.py:28
  261.4 0.0 reduce-scatter.2.cloned.1.call-update
  261.5 0.6 broadcast_multiply_fusion
  262.1 102.4 %all-reduce.2.cloned.1.call-done = f32[8,4096]{1,0:T(8,128)} async-done(((f32[8,4096]{1,0:T(8,128)}), f32[8,4096]{1,0:T(8,128)}) %all-reduce.2.cloned.1.call-update) | async-done | bytes 131088 | tf_op jit(solution)/shard_map/psum | solution.py:53
  364.5 0.0 copy-start.2
  364.5 11.5 %fusion = bf16[1,512,4096]{2,1,0:T(8,128)(2,1)} fusion(f32[512,4096]{1,0:T(8,128)} %copy-done.1, f32[8,512]{1,0:T(8,128)S(1)} %stack.2, f32[8,4096]{1,0:T(8,128)} %all-reduce.2.cloned.1.call-done), kind=kOutput, calls=%fused_computation.2 | convolution fusion | flops 205553664 | bytes 12730368 | tf_op jit(solution)/shard_map/dot_general | solution.py:54
  376.0 0.0 copy-done.2
  376.0 0.7 multiply_bitcast_fusion
  376.7 45.7 %reduce-scatter.2.cloned.1.call-done = f32[32,4096]{1,0:T(8,128)} async-done(((f32[256,4096]{1,0:T(8,128)}), f32[32,4096]{1,0:T(8,128)}) %reduce-scatter.2.cloned.1.call-update) | async-done | bytes 524304 | tf_op jit(solution)/shard_map/reduce_scatter | solution.py:27
  422.4 1.8 convert_element_type.12
  (2 shorter events, 0.1 us)
Async XLA Ops:
  7.2 43.9 %copy-start = (bf16[256,512]{1,0:T(8,128)(2,1)S(1)}, bf16[256,512]{1,0:T(8,128)(2,1)}, u32[]{:S(2)}) copy-start(bf16[256,512]{1,0:T(8,128)(2,1)} %param.5) | copy-start | bytes 786436
  7.2 43.9 %all-gather.2.cloned.1.call-start = ((), (), s32[]{:S(2)}) async-start(), calls=%async_computation.2 | async-start | bytes 2359296 | tf_op jit(solution)/shard_map/all_gather | solution.py:36
  7.9 50.5 %copy-start.3 = (f32[1,8,4096]{2,1,0:T(8,128)S(1)}, f32[1,8,4096]{2,1,0:T(8,128)}, u32[]{:S(2)}) copy-start(f32[1,8,4096]{2,1,0:T(8,128)} %param.9) | copy-start | bytes 393220
  7.9 356.6 %all-reduce.2.cloned.1.call-start = ((), (), s32[]{:S(2)}) async-start(), calls=%async_computation.3 | async-start | bytes 262144 | tf_op jit(solution)/shard_map/psum | solution.py:53
  55.2 3.2 copy-start.1
  255.8 166.6 %reduce-scatter.2.cloned.1.call-start = ((), (), s32[]{:S(2)}) async-start(), calls=%async_computation.1 | async-start | bytes 4718592 | tf_op jit(solution)/shard_map/reduce_scatter | solution.py:27
  364.5 11.5 %copy-start.2 = (f32[8,4096]{1,0:T(8,128)S(1)}, f32[8,4096]{1,0:T(8,128)}, u32[]{:S(2)}) copy-start(f32[8,4096]{1,0:T(8,128)} %all-reduce.2.cloned.1.call-done) | copy-start | bytes 393220
Sparse Core Ops, SparseCore 0:
  9.8 41.1 all-gather.1
  255.9 108.5 all-reduce.1
  367.2 55.1 reduce-scatter.1
where the time goes:
time: 432 us; the launch traced here: 431 us
  waiting for transfers between devices  192 us (44%)
  blocking collectives  123 us (28%)
  other arithmetic  57.8 us (13%)
  matrix products  35.2 us (8%)
  between operations  19.1 us (4%)
    psum x1, blocking collectives, shards(): sketch = lax.psum(sketch, 'dp')  123 us
    psum x1, waiting for transfers between devices, shards(): coefficients = lax.psum(coefficients, 'dp') / replica_count  102 us
    reduce_scatter x1, waiting for transfers between devices, shards(): lax.psum_scatter(jnp.dot(token_rows, weight, preferred_element_type=jnp.f...  45.7 us
    all_gather x1, waiting for transfers between devices, shards(): lax.all_gather(out_grad, 'tensor', axis=0, tiled=True)  43.1 us
    reduce_sum x10, other arithmetic, gram_schmidt(): vector = vector - jnp.sum(vector * earlier) * earlier  29.3 us
    mul x1, other arithmetic, gram_schmidt(): vector = vector * lax.rsqrt(jnp.sum(vector * vector) + epsilon)  17.4 us
    dot_general x1, matrix products, shards(): lax.dot_general(unit_rows, coefficients, (((0,), (0,)), ((), ())), precis...  11.5 us
  transfers between devices with their start and end apart: 3, of which 3 were waited for; matrix products, arithmetic and copies ran while one was open for 4% of the time, Pallas kernels for 0%

commit v1 on v0

v1 whole, which is shorter than its diff:
```python
import functools
import math

import jax
import jax.numpy as jnp
from jax import lax
from jax.experimental import pallas as pl
from jax.experimental.pallas import tpu as pltpu
from jax.sharding import PartitionSpec as P

MESH = pl.DeviceIdType.MESH
F32 = jnp.float32
BF16 = jnp.bfloat16
EPSILON = 1e-06
TILE = 512
XS, YS, CORES = 4, 4, 2
PLANE = XS * CORES
DO_G, DO_RS, DO_AR = True, True, True


def nn(a, b):
    return lax.dot_general(a, b, (((1,), (0,)), ((), ())), preferred_element_type=F32)


def nt(a, b):
    return lax.dot_general(a, b, (((1,), (1,)), ((), ())), preferred_element_type=F32)


def pieces(v):
    high = v.astype(BF16).astype(F32)
    rest = v - high
    middle = rest.astype(BF16).astype(F32)
    return high, middle, rest - middle


def split3(v):
    return jnp.concatenate(pieces(v), axis=0).astype(BF16)


def sum3(v):
    n = v.shape[0] // 3
    return v[:n] + v[n : 2 * n] + v[2 * n :]


def orthonormal(v):
    rows = lax.broadcasted_iota(jnp.int32, (v.shape[0], 1), 0)
    for i in range(v.shape[0]):
        row = v[i : i + 1]
        dots = jnp.sum(v * row, axis=1, keepdims=True)
        scale = lax.rsqrt(dots[i : i + 1] + EPSILON)
        unit = row * scale
        v = jnp.where(rows == i, unit, jnp.where(rows > i, v - (dots * scale) * unit, v))
    return v


def main_kernel(
    x_hbm, w_hbm, g_hbm, e_hbm, wc_ref,
    out_ref, basis_ref, coef_ref, g_out, lhs_ref, u_ref,
    x_ref, w_ref, e_ref, gbuf, part, rbuf, wc3_ref, se_ref, cbuf,
    abuf, bbuf, abuf2, bbuf2, sk_src,
    lsem, g_send, g_recv, rs_send, rs_recv, sk_send, sk_recv, cf_send, cf_recv,
):
    n = 8
    me = lax.axis_index("tensor")
    dp = lax.axis_index("dp")
    y, xc = dp // PLANE, dp % PLANE
    z_to = [lax.rem(me + 1, n), lax.rem(me + n - 1, n)]
    sign = (1, -1)
    a_to = [y * PLANE + lax.rem(xc + k, PLANE) for k in range(PLANE)]
    b_to = [lax.rem(y + k, YS) * PLANE + xc for k in range(YS)]

    lx = pltpu.make_async_copy(x_hbm, x_ref, lsem.at[0])
    lw = pltpu.make_async_copy(w_hbm, w_ref, lsem.at[1])
    le = pltpu.make_async_copy(e_hbm, e_ref, lsem.at[2])
    own = pl.ds(pl.multiple_of(me * 32, 32), 32)
    lg = pltpu.make_async_copy(g_hbm, gbuf.at[own], lsem.at[3])
    lg.start()
    lx.start()
    lw.start()
    le.start()

    barrier = pltpu.get_barrier_semaphore()
    for z in z_to:
        pl.semaphore_signal(barrier, inc=1, device_id={"tensor": z}, device_id_type=MESH)
    for d in a_to[1:] + b_to[1:]:
        pl.semaphore_signal(barrier, inc=1, device_id={"dp": d}, device_id_type=MESH)
    pl.semaphore_wait(barrier, 2 + (PLANE - 1) + (YS - 1))

    def steps(d, h):
        return 4 if d == h else 3

    def g_copy(d, h, s):
        block = lax.rem(me - sign[d] * s + n, n)
        at = pl.ds(pl.multiple_of(block * 32 + h * 16, 16), 16)
        return pltpu.make_async_remote_copy(
            src_ref=gbuf.at[at], dst_ref=gbuf.at[at],
            send_sem=g_send.at[d, h, s], recv_sem=g_recv.at[d, h, s],
            device_id={"tensor": z_to[d]}, device_id_type=MESH)

    def g_step(s):
        for h in range(2):
            for d in range(2):
                if s > 0 and s - 1 < steps(d, h):
                    g_copy(d, h, s - 1).wait_recv()
                if s < steps(d, h):
                    g_copy(d, h, s).start()

    def rs_copy(d, q, s):
        k = steps(d, q // 2)
        dest = lax.rem(me + sign[d] * (k - s) + n, n)
        at = pl.ds(pl.multiple_of(dest * 32, 32), 32)
        cols = pl.ds(q * 1024, 1024)
        return pltpu.make_async_remote_copy(
            src_ref=part.at[at, cols], dst_ref=rbuf.at[d, s, :, cols],
            send_sem=rs_send.at[d, q, s], recv_sem=rs_recv.at[d, q, s],
            device_id={"tensor": z_to[d]}, device_id_type=MESH)

    def rs_step(s, qs=range(4)):
        for q in qs:
            for d in range(2):
                k = steps(d, q // 2)
                cols = pl.ds(q * 1024, 1024)
                if s > 0 and s - 1 < k:
                    rs_copy(d, q, s - 1).wait_recv()
                    dest = lax.rem(me + sign[d] * (k - s) + n, n)
                    at = pl.ds(pl.multiple_of(dest * 32, 32), 32)
                    part[at, cols] += rbuf[d, s - 1, :, cols]
                if s < k:
                    rs_copy(d, q, s).start()

    lg.wait()
    if DO_G:
        g_step(0)
    lx.wait()
    lw.wait()

    @pl.loop(0, 4096, step=TILE)
    def _(c):
        cols = pl.ds(pl.multiple_of(c, TILE), TILE)
        part[:, cols] = nn(x_ref[...], w_ref[:, cols])

    if DO_G:
        g_step(1)
    le.wait()
    if DO_AR:
        wc3_ref[...] = split3(wc_ref[...])
        lhs_ref[...] = x_ref[...].T
        se_ref[...] = jnp.zeros_like(se_ref)

        @pl.loop(0, 4096, step=TILE)
        def _(c):
            cols = pl.ds(pl.multiple_of(c, TILE), TILE)
            se_ref[...] += nt(wc3_ref[:, cols], e_ref[:, cols])

    if DO_G:
        g_step(2)
        g_step(3)
    if DO_RS:
        rs_step(0)
    if DO_G:
        g_step(4)
    lgo = pltpu.make_async_copy(gbuf, g_out, lsem.at[4])
    lgo.start()

    if DO_AR:
        t3 = jnp.zeros((24, 256), F32)
        for c in range(0, 4096, TILE):
            t3 += nt(wc3_ref[:, c : c + TILE], gbuf[:, c : c + TILE])
        sketch = sum3(se_ref[...]) + sum3(nn(split3(sum3(t3)), x_ref[...]))

        def a_copy(k, src, dst, send, recv):
            return pltpu.make_async_remote_copy(
                src_ref=src, dst_ref=dst, send_sem=send.at[k], recv_sem=recv.at[k],
                device_id={"dp": a_to[k]}, device_id_type=MESH)

        def b_copy(k, src, dst, send, recv):
            return pltpu.make_async_remote_copy(
                src_ref=src, dst_ref=dst, send_sem=send.at[PLANE + k], recv_sem=recv.at[PLANE + k],
                device_id={"dp": b_to[k]}, device_id_type=MESH)

        ks_a, ks_b = range(1, PLANE), range(1, YS)
        sk_src[0] = sketch
        copies = [a_copy(k, sk_src.at[0], abuf.at[xc], sk_send, sk_recv) for k in ks_a]
        for c in copies:
            c.start()
        abuf[xc] = sketch
        for c in copies:
            c.wait_recv()
        total = abuf[0]
        for k in range(1, PLANE):
            total += abuf[k]
        sk_src[1] = total
        copies2 = [b_copy(k, sk_src.at[1], bbuf.at[y], sk_send, sk_recv) for k in ks_b]
        for c in copies2:
            c.start()
        bbuf[y] = total
        for c in copies2:
            c.wait_recv()
        total = bbuf[0]
        for k in range(1, YS):
            total += bbuf[k]
        for c in copies + copies2:
            c.wait_send()
        unit = orthonormal(total)
        basis_ref[...] = unit * math.sqrt(512)
        u_ref[...] = unit
        if DO_RS:
            rs_step(1, [0, 1])
        u3 = split3(unit)
        v3 = split3(sum3(nt(u3, x_ref[...])))

        def slab(j):
            return pl.ds(pl.multiple_of(j * 512, 512), 512)

        @pl.loop(0, 4096, step=TILE)
        def _(c):
            cols = pl.ds(pl.multiple_of(c, TILE), TILE)
            cbuf[:, cols] = sum3(nn(u3, e_ref[:, cols]) + nn(v3, gbuf[:, cols]))

        copies = [a_copy(k, cbuf.at[:, slab(lax.rem(xc + k, PLANE))], abuf2.at[xc], cf_send.at[0], cf_recv.at[0]) for k in ks_a]
        for c in copies:
            c.start()
        abuf2[xc] = cbuf[:, slab(xc)]
        for c in copies:
            c.wait_recv()
        total = abuf2[0]
        for k in range(1, PLANE):
            total += abuf2[k]
        for k in range(YS):
            sk_src[2, :, k * 128 : k * 128 + 128] = total[:, k * 128 : k * 128 + 128]

        def piece(j):
            return pl.ds(pl.multiple_of(j * 128, 128), 128)

        copies2 = [b_copy(k, sk_src.at[2, :, piece(lax.rem(y + k, YS))], bbuf2.at[y], cf_send.at[0], cf_recv.at[0]) for k in ks_b]
        for c in copies2:
            c.start()
        bbuf2[y] = sk_src[2, :, piece(y)]
        for c in copies2:
            c.wait_recv()
        if DO_RS:
            rs_step(1, [2, 3])
        for c in copies + copies2:
            c.wait_send()
        total = bbuf2[0]
        for k in range(1, YS):
            total += bbuf2[k]
        total = total * (1.0 / 32)
        mine = pl.ds(pl.multiple_of(xc * 512 + y * 128, 128), 128)
        coef_ref[:, mine] = total
        copies = [b_copy(k, coef_ref.at[:, mine], coef_ref.at[:, mine], cf_send.at[1], cf_recv.at[1]) for k in ks_b]
        for c in copies:
            c.start()
        for c in copies:
            c.wait_recv()
        copies2 = [a_copy(k, coef_ref.at[:, slab(xc)], coef_ref.at[:, slab(xc)], cf_send.at[1], cf_recv.at[1]) for k in ks_a]
        for c in copies2:
            c.start()
        for c in copies2:
            c.wait_recv()
        for c in copies + copies2:
            c.wait_send()
    elif DO_RS:
        rs_step(1)
    if DO_RS:
        rs_step(2)
        rs_step(3)
        rs_step(4)
    out_ref[...] = part[own, :].astype(BF16)
    if DO_G:
        for d in range(2):
            for h in range(2):
                for s in range(steps(d, h)):
                    g_copy(d, h, s).wait_send()
    if DO_RS:
        for d in range(2):
            for q in range(4):
                for s in range(steps(d, q // 2)):
                    rs_copy(d, q, s).wait_send()
    lgo.wait()


def error_kernel(x_ref, u_ref, c_ref, e_ref, g_ref, o_ref):
    c0, c1, c2 = pieces(c_ref[...])
    u0, u1, u2 = pieces(u_ref[...])
    right = jnp.concatenate([c0, c1, c0, c2, c0, c1], axis=0).astype(BF16)
    left = jnp.concatenate([u0, u0, u1, u0, u2, u1], axis=0).T.astype(BF16)
    low = nn(left, right)
    o_ref[...] = (e_ref[...].astype(F32) + nn(x_ref[...], g_ref[...]) - low).astype(BF16)


def shards(inputs, weight, out_grad, error_feedback, warm_coeffs):
    S = jax.ShapeDtypeStruct
    V = pl.BlockSpec(memory_space=pltpu.VMEM)
    A = pl.BlockSpec(memory_space=pl.ANY)
    D = pltpu.SemaphoreType.DMA
    out, basis, coef, g_all, xt, unit = pl.pallas_call(
        main_kernel,
        out_shape=(S((32, 4096), BF16), S((8, 512), F32), S((8, 4096), F32), S((256, 4096), BF16),
                   S((512, 256), BF16), S((8, 512), F32)),
        in_specs=[A, A, A, A, V],
        out_specs=(V, V, V, A, V, V),
        scratch_shapes=[
            pltpu.VMEM((256, 512), BF16),
            pltpu.VMEM((512, 4096), BF16),
            pltpu.VMEM((512, 4096), BF16),
            pltpu.VMEM((256, 4096), BF16),
            pltpu.VMEM((256, 4096), F32),
            pltpu.VMEM((2, 4, 32, 4096), F32),
            pltpu.VMEM((24, 4096), BF16),
            pltpu.VMEM((24, 512), F32),
            pltpu.VMEM((8, 4096), F32),
            pltpu.VMEM((PLANE, 8, 512), F32),
            pltpu.VMEM((YS, 8, 512), F32),
            pltpu.VMEM((PLANE, 8, 512), F32),
            pltpu.VMEM((YS, 8, 128), F32),
            pltpu.VMEM((3, 8, 512), F32),
            D((5,)),
            D((2, 2, 4)), D((2, 2, 4)),
            D((2, 4, 4)), D((2, 4, 4)),
            D((PLANE + YS,)), D((PLANE + YS,)),
            D((2, PLANE + YS)), D((2, PLANE + YS)),
        ],
        compiler_params=pltpu.CompilerParams(
            collective_id=0, has_side_effects=True, vmem_limit_bytes=48 * 2**20),
    )(inputs, weight, out_grad, error_feedback[0], warm_coeffs[0])
    whole = lambda i: (0, 0)
    cols = lambda i: (0, i)
    err = pl.pallas_call(
        error_kernel,
        grid=(4096 // TILE,),
        out_shape=S((512, 4096), BF16),
        in_specs=[pl.BlockSpec((512, 256), whole), pl.BlockSpec((8, 512), whole), pl.BlockSpec((8, TILE), cols),
                  pl.BlockSpec((512, TILE), cols), pl.BlockSpec((256, TILE), cols)],
        out_specs=pl.BlockSpec((512, TILE), cols),
        compiler_params=pltpu.CompilerParams(vmem_limit_bytes=24 * 2**20),
    )(xt, unit, coef, error_feedback[0], g_all)
    return (out, basis, coef[None], err[None])


def solution(mesh):
    in_specs = (
        P("dp", "tensor"),
        P("tensor", None),
        P(("dp", "tensor"), None),
        P("dp", "tensor", None),
        P("tensor", None, None),
    )
    out_specs = (
        P(("dp", "tensor"), None),
        P(None, "tensor"),
        P("tensor", None, None),
        P("dp", "tensor", None),
    )
    return jax.shard_map(shards, mesh=mesh, in_specs=in_specs, out_specs=out_specs, check_vma=False)
```

time: 432 us -> 93.9 us (0.22)
  waiting for transfers between devices: 192 us -> 0 us
  blocking collectives: 123 us -> 0 us
  Pallas kernels: 0 us -> 88.3 us
  other arithmetic: 57.8 us -> 0 us
  matrix products: 35.2 us -> 0 us
  between operations: 19.1 us -> 0.66 us
    psum x1 -> x0, blocking collectives: 123 us -> none  [shards(): sketch = lax.psum(sketch, 'dp')]
    psum x1 -> x0, waiting for transfers between devices: 102 us -> none  [shards(): coefficients = lax.psum(coefficients, 'dp') / replica_count]
    pallas_call x0 -> x2, Pallas kernels: none -> 88.3 us  [the longest x1 82.3 us: shards(): pl.pallas_call(main_kernel, out_shape=(S((32, 4096), BF16), S((8, 512), F...]
    reduce_scatter x1 -> x0, waiting for transfers between devices: 45.7 us -> none  [shards(): lax.psum_scatter(jnp.dot(token_rows, weight, preferred_element_type=jnp.f...]
    all_gather x1 -> x0, waiting for transfers between devices: 43.1 us -> none  [shards(): lax.all_gather(out_grad, 'tensor', axis=0, tiled=True)]
    reduce_sum x15 -> x0, other arithmetic: 37.4 us -> none  [the longest x10 29.3 us: gram_schmidt(): vector = vector - jnp.sum(vector * earlier) * earlier]
    dot_general x5 -> x0, matrix products: 35.2 us -> none  [the longest x1 11.5 us: shards(): lax.dot_general(unit_rows, coefficients, (((0,), (0,)), ((), ())), precis...]
    mul x2 -> x0, other arithmetic: 18 us -> none  [the longest x1 17.4 us: gram_schmidt(): vector = vector * lax.rsqrt(jnp.sum(vector * vector) + epsilon)]
  transfers between devices with their start and end apart: 3 -> 0, of which waited for: 3 -> 0; matrix products, arithmetic and copies ran while one was open for 4% -> 0% of each run, Pallas kernels for 0% -> 0%
where the time goes in v1:
time: 93.9 us; the launch traced here: 93.7 us
  Pallas kernels  88.3 us (94%)
  local copies, waits for them, and re-layouts  4.76 us (5%)
    pallas_call x1, Pallas kernels, shards(): pl.pallas_call(main_kernel, out_shape=(S((32, 4096), BF16), S((8, 512), F...  82.3 us
    pallas_call x1, Pallas kernels, shards(): pl.pallas_call(error_kernel, grid=(4096 // TILE,), out_shape=S((512, 4096...  5.92 us
    unnamed x11, local copies, waits for them, and re-layouts  4.76 us

profile of v1, /device:TPU:1, one launch (start us, length us, event | category | flops | bytes accessed | tf_op | source)
XLA Modules:
  0.0 93.7 jit_solution(1320843874056784253)
XLA Ops:
  0.6 0.0 copy-start.1
  0.6 0.9 %copy-done.1 = bf16[256,512]{1,0:T(8,128)(2,1)S(1)} copy-done((bf16[256,512]{1,0:T(8,128)(2,1)S(1)}, bf16[256,512]{1,0:T(8,128)(2,1)}, u32[]{:S(2)}) %copy-start.1) | copy-done | bytes 262168
  1.6 0.0 copy-start.2
  1.6 0.9 %copy-done.2 = bf16[32,4096]{1,0:T(8,128)(2,1)S(1)} copy-done((bf16[32,4096]{1,0:T(8,128)(2,1)S(1)}, bf16[32,4096]{1,0:T(8,128)(2,1)}, u32[]{:S(2)}) %copy-start.2) | copy-done | bytes 262168
  2.5 0.0 copy-start.3
  2.5 0.9 copy-done.3
  3.4 0.0 copy-start
  3.4 82.3 %shard_map.84 = (bf16[32,4096]{1,0:T(8,128)(2,1)S(1)}, f32[8,512]{1,0:T(8,128)S(1)}, f32[8,4096]{1,0:T(8,128)S(1)}, bf16[256,4096]{1,0:T(8,128)(2,1)S(1)}, bf16[...) custom-call(bf16[256,512]{1,0:T(8,128)(2,1)S(1)} %copy-done.1, bf16[512,4096]{1,0:T(8,128)(2,1)} %w_hbm.1, ...), custom_call_target="tpu_custom_call" | custom-call | tf_op jit(solution)/shard_map/pallas_call | solution.py:297
  85.8 0.0 copy-done
  85.8 5.9 %shard_map.85 = bf16[512,4096]{1,0:T(8,128)(2,1)} custom-call(bf16[512,256]{1,0:T(8,128)(2,1)S(1)} %get-tuple-element.13.x_ref, f32[8,512]{1,0:T(8,128)S(1)} %get-tuple-element.14.u_ref, f32[8,4096]{1,0:T(8,128)S(1)} %get-tuple-element.12.c_ref, bf16[512,4096]{1,0:T(8,128)(2,1)S(1)} %bitcast.5, bf16[256,4096]{1,0:T(8,128)(2,1)S(1)} %get-tuple-element.15.g_ref), custom_call_target="tpu_custom_call" | custom-call | tf_op jit(solution)/shard_map/pallas_call | solution.py:329
  91.7 0.7 copy.12
  92.4 0.6 copy.13
  93.0 0.7 copy.14
Async XLA Ops:
  0.6 1.0 %copy-start.1 = (bf16[256,512]{1,0:T(8,128)(2,1)S(1)}, bf16[256,512]{1,0:T(8,128)(2,1)}, u32[]{:S(2)}) copy-start(bf16[256,512]{1,0:T(8,128)(2,1)} %x_hbm.1) | copy-start | bytes 786436
  1.6 0.9 %copy-start.2 = (bf16[32,4096]{1,0:T(8,128)(2,1)S(1)}, bf16[32,4096]{1,0:T(8,128)(2,1)}, u32[]{:S(2)}) copy-start(bf16[32,4096]{1,0:T(8,128)(2,1)} %g_hbm.1) | copy-start | bytes 786436
  2.5 0.9 copy-start.3
  3.4 82.4 %copy-start = (bf16[1,512,4096]{2,1,0:T(8,128)(2,1)S(1)}, bf16[1,512,4096]{2,1,0:T(8,128)(2,1)}, u32[]{:S(2)}) copy-start(bf16[1,512,4096]{2,1,0:T(8,128)(2,1)} %param.8) | copy-start | bytes 12582916

commit v2 on v0

v2 whole, which is shorter than its diff:
```python
import functools
import math

import jax
import jax.numpy as jnp
from jax import lax
from jax.experimental import pallas as pl
from jax.experimental.pallas import tpu as pltpu
from jax.sharding import PartitionSpec as P

MESH = pl.DeviceIdType.MESH
F32 = jnp.float32
BF16 = jnp.bfloat16
EPSILON = 1e-06
TILE = 512
PARTS = 4
XS, YS, CORES = 4, 4, 2
PLANE = XS * CORES
DP = YS * PLANE


def nn(a, b):
    return lax.dot_general(a, b, (((1,), (0,)), ((), ())), preferred_element_type=F32)


def nt(a, b):
    return lax.dot_general(a, b, (((1,), (1,)), ((), ())), preferred_element_type=F32)


def pieces(v):
    high = v.astype(BF16).astype(F32)
    rest = v - high
    middle = rest.astype(BF16).astype(F32)
    return high, middle, rest - middle


def split3(v):
    return jnp.concatenate(pieces(v), axis=0).astype(BF16)


def sum3(v):
    n = v.shape[0] // 3
    return v[:n] + v[n : 2 * n] + v[2 * n :]


def orthonormal(v):
    rows = lax.broadcasted_iota(jnp.int32, (v.shape[0], 1), 0)
    for i in range(v.shape[0]):
        row = v[i : i + 1]
        dots = jnp.sum(v * row, axis=1, keepdims=True)
        scale = lax.rsqrt(dots[i : i + 1] + EPSILON)
        unit = row * scale
        v = jnp.where(rows == i, unit, jnp.where(rows > i, v - (dots * scale) * unit, v))
    return v


def main_kernel(
    x_hbm, w_hbm, g_hbm, e_hbm, wc_hbm,
    out_ref, coef_ref, merged_ref, u_ref,
    x_ref, e_ref, gbuf, xa, wp, yacc, yb, wc_ref, wz, w3_ref, gpad, tsrc, tdst, se_ref, xt_ref, cbuf,
    abuf, bbuf, cin, sk_src,
    lsem, g_send, g_recv, xz_send, xz_recv, xy_send, xy_recv, w_send, w_recv, wc_send, wc_recv,
    y_send, y_recv, sk_send, sk_recv, cf_send, cf_recv, c_send, c_recv, p_send, p_recv, k_send, k_recv,
    t_send, t_recv,
):
    n = 8
    me = lax.axis_index("tensor")
    dp = lax.axis_index("dp")
    core = dp % CORES
    chip = dp // CORES
    y, xc = dp // PLANE, dp % PLANE
    xq = xc // CORES
    z_all = [lax.rem(me + k, n) for k in range(n)]
    z_to = [z_all[1], z_all[n - 1]]
    sign = (1, -1)
    a_to = [y * PLANE + lax.rem(xc + k, PLANE) for k in range(PLANE)]
    b_to = [lax.rem(y + k, YS) * PLANE + xc for k in range(YS)]
    d_to = [lax.rem(dp + k, DP) for k in range(DP)]
    chips = [lax.rem(chip + k, XS * YS) for k in range(XS * YS)]
    p_to = [c * CORES + core for c in chips]
    partner = chip * CORES + (1 - core)

    def shifted(axis, r):
        if axis == 0:
            return y * XS + lax.rem(xq + r + XS, XS)
        return lax.rem(y + r + YS, YS) * XS + xq

    own = pl.ds(pl.multiple_of(me * 32, 32), 32)
    mine = pl.ds(pl.multiple_of(chip * 32, 32), 32)
    own_cols = pl.ds(pl.multiple_of(me * 512, 512), 512)
    own_rows = own_cols
    chip_cols = pl.ds(pl.multiple_of(chip * 256, 256), 256)
    lx = pltpu.make_async_copy(x_hbm, x_ref, lsem.at[0])
    lw = pltpu.make_async_copy(w_hbm.at[:, chip_cols], wp.at[own_rows, :], lsem.at[1])
    le = pltpu.make_async_copy(e_hbm, e_ref, lsem.at[2])
    lg = pltpu.make_async_copy(g_hbm, gbuf.at[own], lsem.at[3])
    lc = pltpu.make_async_copy(wc_hbm, wc_ref, lsem.at[5])
    lp = pltpu.make_async_copy(g_hbm, gpad.at[pl.ds(pl.multiple_of(lax.rem(me, 4) * 32, 32), 32)], lsem.at[4])
    for c in (lc, lx, lg, le, lw):
        c.start()

    barrier = pltpu.get_barrier_semaphore()
    for z in z_all[1:]:
        pl.semaphore_signal(barrier, inc=1, device_id={"tensor": z}, device_id_type=MESH)
    for d in d_to[1:]:
        pl.semaphore_signal(barrier, inc=1, device_id={"dp": d}, device_id_type=MESH)
    gpad[...] = jnp.zeros_like(gpad)
    lp.start()
    pl.semaphore_wait(barrier, 7 + 31)

    def settle(ref, sem):
        pltpu.make_async_copy(ref, ref, sem).wait()

    def steps(d, h):
        return 4 if d == h else 3

    def ring_copy(buf, rows, part, cols, send, recv, d, h, s):
        block = lax.rem(me - sign[d] * s + n, n)
        at = pl.ds(pl.multiple_of(block * rows + h * part, part), part)
        return pltpu.make_async_remote_copy(
            src_ref=buf.at[at, cols], dst_ref=buf.at[at, cols],
            send_sem=send, recv_sem=recv.at[d, h, s],
            device_id={"tensor": z_to[d]}, device_id_type=MESH)

    def g_copy(d, h, s):
        return ring_copy(gbuf, 32, 16, slice(None), g_send, g_recv, d, h, s)

    core_cols = pl.ds(pl.multiple_of(core * 128, 128), 128)

    def w_copy(d, h, s):
        return ring_copy(wp, 512, 256, core_cols, w_send, w_recv, d, h, s)

    def wc_copy(d, h, s):
        block = lax.rem(me - sign[d] * (s + 1) + n, n)
        at = pl.ds(pl.multiple_of(block * 512 + h * 256, 256), 256)
        return pltpu.make_async_remote_copy(
            src_ref=wp.at[at, core_cols], dst_ref=wp.at[at, core_cols],
            send_sem=wc_send, recv_sem=wc_recv.at[s],
            device_id={"dp": partner}, device_id_type=MESH)

    def g_step(s):
        for h in range(2):
            for d in range(2):
                if s > 0 and s - 1 < steps(d, h):
                    g_copy(d, h, s - 1).wait_recv()
                if s < steps(d, h):
                    g_copy(d, h, s).start()

    def w_step(s):
        for h in range(2):
            for d in range(2):
                if s > 0 and s - 1 < steps(d, h):
                    w_copy(d, h, s - 1).wait_recv()
                if s < steps(d, h):
                    w_copy(d, h, s).start()
                if s > 0 and s - 1 < steps(d, h):
                    wc_copy(d, h, s - 1).start()

    def xz_copy(k):
        src = pl.ds(pl.multiple_of(z_all[k] * 32, 32), 32)
        return pltpu.make_async_remote_copy(
            src_ref=x_ref.at[src], dst_ref=xa.at[mine, own_cols],
            send_sem=xz_send, recv_sem=xz_recv,
            device_id={"tensor": z_all[k]}, device_id_type=MESH)

    shifts = (0, -1, 1, 2)

    def xy_copy(h, stage, kind):
        first = h
        second = 1 - h
        axis = first if stage == 0 else second
        r = 0 if stage == 0 else shifts[stage - 1]
        b = (0, 0, -1, 1)[kind]
        go = (1, -1, 1, -1)[kind]
        ra, rb = (b, 0) if stage == 0 else (r, b)
        if first == 0:
            rx, ry = ra, rb
        else:
            rx, ry = rb, ra
        block = lax.rem(y + ry + YS, YS) * XS + lax.rem(xq + rx + XS, XS)
        at = pl.ds(pl.multiple_of(block * 32 + h * 16, 16), 16)
        cols = (slice(None), slice(None), pl.ds(0, 2048), pl.ds(2048, 2048))[kind]
        return pltpu.make_async_remote_copy(
            src_ref=xa.at[at, cols], dst_ref=xa.at[at, cols],
            send_sem=xy_send, recv_sem=xy_recv.at[h, stage, min(kind, 2)],
            device_id={"dp": shifted(axis, go) * CORES + core}, device_id_type=MESH)

    def xy_full(h, stage):
        xy_copy(h, stage, 0).start()
        xy_copy(h, stage, 1).start()

    def xy_one(h, stage):
        xy_copy(h, stage, 0).wait_recv()
        xy_copy(h, stage, 2).start()
        if stage == 0:
            xy_full(h, 2)
        xy_copy(h, stage, 1).wait_recv()
        xy_copy(h, stage, 3).start()
        if stage == 0:
            xy_full(h, 3)

    def xy_two(h, stage):
        settle(xa.at[pl.ds(0, 16)], xy_recv.at[h, stage, 2])
        if stage == 0:
            xy_full(h, 4)

    def y_copy(k):
        src = pl.ds(pl.multiple_of(chips[k] * 32, 32), 32)
        return pltpu.make_async_remote_copy(
            src_ref=yb.at[src], dst_ref=out_ref.at[:, chip_cols],
            send_sem=y_send, recv_sem=y_recv,
            device_id={"dp": p_to[k]}, device_id_type=MESH)

    def c_copy(k):
        return pltpu.make_async_remote_copy(
            src_ref=wc_ref.at[:, pl.ds(pl.multiple_of(dp * 128, 128), 128)],
            dst_ref=wz.at[core, y, xq, pl.ds(pl.multiple_of(me * 8, 8), 8)],
            send_sem=c_send, recv_sem=c_recv,
            device_id={"tensor": z_all[k]}, device_id_type=MESH)

    def p_copy(h, phase, k):
        rows = pl.ds(h * 32, 32)
        axis = h if phase == 0 else 1 - h
        if phase == 0:
            at = wz.at[core, y, xq, rows]
        elif axis == 1:
            at = wz.at[core, y, :, rows]
        else:
            at = wz.at[core, :, xq, rows]
        return pltpu.make_async_remote_copy(
            src_ref=at, dst_ref=at, send_sem=p_send.at[h, phase], recv_sem=p_recv.at[h, phase],
            device_id={"dp": shifted(axis, k) * CORES + core}, device_id_type=MESH)

    def k_copy(h):
        at = wz.at[core, :, :, pl.ds(h * 32, 32)]
        return pltpu.make_async_remote_copy(
            src_ref=at, dst_ref=at, send_sem=k_send.at[h], recv_sem=k_recv.at[h],
            device_id={"dp": partner}, device_id_type=MESH)

    def t_copy(k):
        return pltpu.make_async_remote_copy(
            src_ref=tsrc.at[z_all[k]], dst_ref=tdst.at[me], send_sem=t_send, recv_sem=t_recv,
            device_id={"tensor": z_all[k]}, device_id_type=MESH)

    def a_copy(k, src, dst, send, recv):
        return pltpu.make_async_remote_copy(
            src_ref=src, dst_ref=dst, send_sem=send.at[0], recv_sem=recv.at[0],
            device_id={"dp": a_to[k]}, device_id_type=MESH)

    def b_copy(k, src, dst, send, recv):
        return pltpu.make_async_remote_copy(
            src_ref=src, dst_ref=dst, send_sem=send.at[1], recv_sem=recv.at[1],
            device_id={"dp": b_to[k]}, device_id_type=MESH)

    lc.wait()
    for k in range(1, n):
        c_copy(k).start()
    wz[core, y, xq, pl.ds(pl.multiple_of(me * 8, 8), 8)] = wc_ref[:, pl.ds(pl.multiple_of(dp * 128, 128), 128)]
    lx.wait()
    lg.wait()
    xa[mine, own_cols] = x_ref[own, :]
    xt_ref[...] = x_ref[...].T
    settle(wz.at[0, 0, 0, pl.ds(0, 56)], c_recv)
    for h in range(2):
        for k in range(1, 4):
            p_copy(h, 0, k).start()
    for k in range(1, n):
        xz_copy(k).start()
    g_step(0)
    le.wait()
    se_ref[...] = jnp.zeros_like(se_ref)

    def sketch_error(low, high):
        @pl.loop(low, high, step=TILE)
        def _(c):
            cols = pl.ds(pl.multiple_of(c, TILE), TILE)
            se_ref[...] += nt(split3(wc_ref[:, cols]), e_ref[:, cols])

    sketch_error(0, 2048)
    for h in range(2):
        settle(wz.at[0, 0, pl.ds(0, 3), pl.ds(0, 32)], p_recv.at[h, 0])
        for k in range(1, 4):
            p_copy(h, 1, k).start()
    sketch_error(2048, 4096)
    for h in range(2):
        settle(wz.at[0, pl.ds(0, 3), :, pl.ds(0, 32)], p_recv.at[h, 1])
        k_copy(h).start()
    for h in range(2):
        k_copy(h).wait_recv()
    for d in range(DP):
        w3_ref[:, d * 128 : d * 128 + 128] = split3(wz[d % CORES, d // PLANE, d % PLANE // CORES])
    lp.wait()
    partial = sum3(nt(w3_ref[...], gpad[...]))
    for t in range(n):
        tsrc[t] = partial[t * 8 : t * 8 + 8]
    for k in range(1, n):
        t_copy(k).start()
    tdst[me] = tsrc[me]
    settle(xa.at[pl.ds(0, 32), pl.ds(0, 3584)], xz_recv)
    for h in range(2):
        xy_full(h, 0)
    for h in range(2):
        xy_full(h, 1)
    g_step(1)
    settle(tdst.at[pl.ds(0, 7)], t_recv)
    tokens = jnp.concatenate(
        [tdst[0] + tdst[1] + tdst[2] + tdst[3], tdst[4] + tdst[5] + tdst[6] + tdst[7]], axis=1)
    sketch = sum3(se_ref[...]) + sum3(nn(split3(tokens), x_ref[...]))
    ks_a, ks_b = range(1, PLANE), range(1, YS)
    sk_src[0] = sketch
    for k in ks_a:
        a_copy(k, sk_src.at[0], abuf.at[xc], sk_send, sk_recv).start()
    abuf[xc] = sketch
    for h in range(2):
        xy_one(h, 0)
    for h in range(2):
        xy_one(h, 1)
    g_step(2)
    settle(abuf.at[pl.ds(0, PLANE - 1)], sk_recv.at[0])
    total = abuf[0]
    for k in range(1, PLANE):
        total += abuf[k]
    sk_src[1] = total
    for k in ks_b:
        b_copy(k, sk_src.at[1], bbuf.at[y], sk_send, sk_recv).start()
    bbuf[y] = total
    for h in range(2):
        xy_two(h, 0)
    for h in range(2):
        xy_two(h, 1)
    g_step(3)
    lw.wait()
    w_step(0)
    settle(bbuf.at[pl.ds(0, YS - 1)], sk_recv.at[1])
    total = bbuf[0]
    for k in range(1, YS):
        total += bbuf[k]
    unit = orthonormal(total)
    u_ref[...] = unit
    u3 = split3(unit)
    v3 = split3(sum3(nt(u3, x_ref[...])))

    @pl.loop(0, 4096, step=TILE)
    def _(c):
        cols = pl.ds(pl.multiple_of(c, TILE), TILE)
        cbuf[:, cols] = sum3(nn(u3, e_ref[:, cols]))

    for h in range(2):
        xy_one(h, 2)
    for h in range(2):
        xy_one(h, 3)
    g_step(4)

    @pl.loop(0, 4096, step=TILE)
    def _(c):
        cols = pl.ds(pl.multiple_of(c, TILE), TILE)
        cbuf[:, cols] += sum3(nn(v3, gbuf[:, cols]))

    def piece(j):
        return pl.ds(pl.multiple_of(j * 128, 128), 128)

    my_piece = piece(dp)

    def r_copy(k):
        return pltpu.make_async_remote_copy(
            src_ref=cbuf.at[:, piece(d_to[k])], dst_ref=cin.at[dp],
            send_sem=cf_send.at[0], recv_sem=cf_recv.at[0],
            device_id={"dp": d_to[k]}, device_id_type=MESH)

    def s_copy(k):
        return pltpu.make_async_remote_copy(
            src_ref=coef_ref.at[:, my_piece], dst_ref=coef_ref.at[:, my_piece],
            send_sem=cf_send.at[1], recv_sem=cf_recv.at[1],
            device_id={"dp": d_to[k]}, device_id_type=MESH)

    for k in range(1, DP):
        r_copy(k).start()
    cin[dp] = cbuf[:, my_piece]
    w_step(1)
    for h in range(2):
        xy_one(h, 4)

    def merge(low, high):
        @pl.loop(low, high, step=TILE)
        def _(c):
            cols = pl.ds(pl.multiple_of(c, TILE), TILE)
            merged_ref[:, cols] = e_ref[:, cols].astype(F32) + nn(xt_ref[...], gbuf[:, cols])

    def product(shift, first=False):
        t = lax.rem(me + shift + n, n)
        at = pl.ds(pl.multiple_of(t * 512, 512), 512)

        @pl.loop(0, 512, step=256)
        def _(r):
            rows = pl.ds(pl.multiple_of(r, 256), 256)
            part = nn(xa[rows, at], wp[at, :])
            yacc[rows, :] = part if first else yacc[rows, :] + part

    def w_ready(s):
        settle(wp.at[pl.ds(0, 1024 if s < 3 else 512), pl.ds(0, 128)], wc_recv.at[s])

    merge(0, 2048)
    w_step(2)
    settle(cin.at[pl.ds(0, DP - 1)], cf_recv.at[0])
    total = cin[0]
    for k in range(1, DP):
        total += cin[k]
    coef_ref[:, my_piece] = total * (1.0 / 32)
    for k in range(1, DP):
        s_copy(k).start()
    merge(2048, 4096)
    for h in range(2):
        for stage in range(2, 5):
            xy_two(h, stage)
    product(0, True)
    w_step(3)
    for s in range(2):
        w_ready(s)
        product(s + 1)
        product(-s - 1)
    w_step(4)
    w_ready(2)
    product(3)
    product(-3)
    w_ready(3)
    product(4)
    yb[...] = yacc[...].astype(BF16)
    for k in range(1, XS * YS):
        y_copy(k).start()
    out_ref[:, chip_cols] = yb[mine, :]
    settle(coef_ref.at[:, pl.ds(0, 128 * (DP - 1))], cf_recv.at[1])
    settle(cbuf.at[:, pl.ds(0, 128 * (DP - 1))], cf_send.at[0])
    settle(coef_ref.at[:, pl.ds(0, 128 * (DP - 1))], cf_send.at[1])
    settle(abuf.at[pl.ds(0, PLANE - 1)], sk_send.at[0])
    settle(bbuf.at[pl.ds(0, YS - 1)], sk_send.at[1])
    settle(xa.at[pl.ds(0, 32), pl.ds(0, 3584)], xz_send)
    settle(wz.at[0, 0, 0, pl.ds(0, 56)], c_send)
    settle(tdst.at[pl.ds(0, 7)], t_send)
    for h in range(2):
        k_copy(h).wait_send()
        settle(wz.at[0, 0, pl.ds(0, 3), pl.ds(0, 32)], p_send.at[h, 0])
        settle(wz.at[0, pl.ds(0, 3), :, pl.ds(0, 32)], p_send.at[h, 1])
    settle(gbuf.at[pl.ds(0, 224)], g_send)
    settle(wp.at[pl.ds(0, 3584), pl.ds(0, 128)], w_send)
    settle(wp.at[pl.ds(0, 3584), pl.ds(0, 128)], wc_send)
    settle(xa.at[pl.ds(0, 480)], xy_send)
    settle(yb.at[pl.ds(0, 480)], y_recv)
    settle(yb.at[pl.ds(0, 480)], y_send)


def error_kernel(m_ref, u_ref, c_ref, y_ref, o_hbm, out_hbm, coef_hbm, basis_hbm, o_ref, basis_ref, sem, o_sem):
    basis_ref[...] = u_ref[...] * math.sqrt(512)
    through = [pltpu.make_async_copy(a, b, sem.at[i]) for i, (a, b) in enumerate(
        ((y_ref, out_hbm), (c_ref, coef_hbm), (basis_ref, basis_hbm)))]
    for c in through:
        c.start()
    u0, u1, u2 = pieces(u_ref[...])
    left = jnp.concatenate([u0, u0, u1, u0, u2, u1], axis=0).T.astype(BF16)
    width = 4096 // PARTS
    stores = []
    for i in range(PARTS):
        cols = pl.ds(i * width, width)
        c0, c1, c2 = pieces(c_ref[:, cols])
        right = jnp.concatenate([c0, c1, c0, c2, c0, c1], axis=0).astype(BF16)
        for r in range(0, 512, 256):
            for c in range(0, width, 256):
                at = (slice(r, r + 256), pl.ds(i * width + c, 256))
                o_ref[at] = (m_ref[at] - nn(left[r : r + 256], right[:, c : c + 256])).astype(BF16)
        stores.append(pltpu.make_async_copy(o_ref.at[:, cols], o_hbm.at[:, cols], o_sem.at[i]))
        stores[i].start()
    for c in stores + through:
        c.wait()


def shards(inputs, weight, out_grad, error_feedback, warm_coeffs):
    S = jax.ShapeDtypeStruct
    V = pl.BlockSpec(memory_space=pltpu.VMEM)
    A = pl.BlockSpec(memory_space=pl.ANY)
    D = pltpu.SemaphoreType.DMA
    VM = pltpu.VMEM
    hbm = lambda v: pltpu.with_memory_space_constraint(v, pltpu.HBM)
    operands = [hbm(v) for v in (inputs, weight, out_grad, error_feedback[0], warm_coeffs[0])]
    out, coef, merged, unit = pl.pallas_call(
        main_kernel,
        out_shape=(VM((32, 4096), BF16), VM((8, 4096), F32), VM((512, 4096), F32), VM((8, 512), F32)),
        in_specs=[A, A, A, A, A],
        out_specs=(V, V, V, V),
        scratch_shapes=[
            VM((256, 512), BF16),
            VM((512, 4096), BF16),
            VM((256, 4096), BF16),
            VM((512, 4096), BF16),
            VM((4096, 256), BF16),
            VM((512, 256), F32),
            VM((512, 256), BF16),
            VM((8, 4096), F32),
            VM((CORES, YS, XS, 64, 128), F32),
            VM((192, 4096), BF16),
            VM((128, 4096), BF16),
            VM((8, 8, 128), F32),
            VM((8, 8, 128), F32),
            VM((24, 512), F32),
            VM((512, 256), BF16),
            VM((8, 4096), F32),
            VM((PLANE, 8, 512), F32),
            VM((YS, 8, 512), F32),
            VM((DP, 8, 128), F32),
            VM((2, 8, 512), F32),
            D((6,)),
            D, D((2, 2, 4)),
            D, D,
            D, D((2, 5, 3)),
            D, D((2, 2, 4)),
            D, D((4,)),
            D, D,
            D((2,)), D((2,)),
            D((2,)), D((2,)),
            D, D,
            D((2, 2)), D((2, 2)),
            D((2,)), D((2,)),
            D, D,
        ],
        compiler_params=pltpu.CompilerParams(
            collective_id=0, has_side_effects=True, vmem_limit_bytes=40 * 2**20),
    )(*operands)
    err, out, coef, basis = pl.pallas_call(
        error_kernel,
        out_shape=(S((512, 4096), BF16), S((32, 4096), BF16), S((8, 4096), F32), S((8, 512), F32)),
        in_specs=[V, V, V, V],
        out_specs=(A, A, A, A),
        scratch_shapes=[VM((512, 4096), BF16), VM((8, 512), F32), D((3,)), D((PARTS,))],
        compiler_params=pltpu.CompilerParams(vmem_limit_bytes=24 * 2**20),
    )(merged, unit, coef, out)
    return (out, basis, coef[None], err[None])


def solution(mesh):
    in_specs = (
        P("dp", "tensor"),
        P("tensor", None),
        P(("dp", "tensor"), None),
        P("dp", "tensor", None),
        P("tensor", None, None),
    )
    out_specs = (
        P(("dp", "tensor"), None),
        P(None, "tensor"),
        P("tensor", None, None),
        P("dp", "tensor", None),
    )
    return jax.shard_map(shards, mesh=mesh, in_specs=in_specs, out_specs=out_specs, check_vma=False)
```

time: 432 us -> 74.3 us (0.17)
  waiting for transfers between devices: 192 us -> 0 us
  blocking collectives: 123 us -> 0 us
  Pallas kernels: 0 us -> 73.5 us
  other arithmetic: 57.8 us -> 0 us
  matrix products: 35.2 us -> 0 us
  between operations: 19.1 us -> 0.64 us
    psum x1 -> x0, blocking collectives: 123 us -> none  [shards(): sketch = lax.psum(sketch, 'dp')]
    psum x1 -> x0, waiting for transfers between devices: 102 us -> none  [shards(): coefficients = lax.psum(coefficients, 'dp') / replica_count]
    pallas_call x0 -> x2, Pallas kernels: none -> 73.5 us  [the longest x1 70.9 us: shards(): pl.pallas_call(main_kernel, out_shape=(VM((32, 4096), BF16), VM((8, 4096)...]
    reduce_scatter x1 -> x0, waiting for transfers between devices: 45.7 us -> none  [shards(): lax.psum_scatter(jnp.dot(token_rows, weight, preferred_element_type=jnp.f...]
    all_gather x1 -> x0, waiting for transfers between devices: 43.1 us -> none  [shards(): lax.all_gather(out_grad, 'tensor', axis=0, tiled=True)]
    reduce_sum x15 -> x0, other arithmetic: 37.4 us -> none  [the longest x10 29.3 us: gram_schmidt(): vector = vector - jnp.sum(vector * earlier) * earlier]
    dot_general x5 -> x0, matrix products: 35.2 us -> none  [the longest x1 11.5 us: shards(): lax.dot_general(unit_rows, coefficients, (((0,), (0,)), ((), ())), precis...]
    mul x2 -> x0, other arithmetic: 18 us -> none  [the longest x1 17.4 us: gram_schmidt(): vector = vector * lax.rsqrt(jnp.sum(vector * vector) + epsilon)]
  transfers between devices with their start and end apart: 3 -> 0, of which waited for: 3 -> 0; matrix products, arithmetic and copies ran while one was open for 4% -> 0% of each run, Pallas kernels for 0% -> 0%
where the time goes in v2:
time: 74.3 us; the launch traced here: 74.2 us
  Pallas kernels  73.5 us (99%)
    pallas_call x1, Pallas kernels, shards(): pl.pallas_call(main_kernel, out_shape=(VM((32, 4096), BF16), VM((8, 4096)...  70.9 us
    pallas_call x1, Pallas kernels, shards(): pl.pallas_call(error_kernel, out_shape=(S((512, 4096), BF16), S((32, 4096...  2.68 us

profile of v2, /device:TPU:1, one launch (start us, length us, event | category | flops | bytes accessed | tf_op | source)
XLA Modules:
  0.0 74.2 jit_solution(8189942556701574415)
XLA Ops:
  0.6 70.9 %shard_map.84 = (bf16[32,4096]{1,0:T(8,128)(2,1)S(1)}, f32[8,4096]{1,0:T(8,128)S(1)}, f32[512,4096]{1,0:T(8,128)S(1)}, f32[8,512]{1,0:T(8,128)S(1)}) custom-call(bf16[256,512]{1,0:T(8,128)(2,1)} %x_hbm.1, bf16[512,4096]{1,0:T(8,128)(2,1)} %w_hbm.1, bf16[32,4096]{1,0:T(8,128)(2,1)} %g_hbm.1, bf16[512,4096]{1,0:T(8,128)(2,1)} %bitcast.4, f32[8,4096]{1,0:T(8,128)} %bitcast.5), custom_call_target="tpu_custom_call" | custom-call | tf_op jit(solution)/shard_map/pallas_call | solution.py:483
  71.5 2.7 %shard_map.85 = (bf16[512,4096]{1,0:T(8,128)(2,1)}, bf16[32,4096]{1,0:T(8,128)(2,1)}, f32[8,4096]{1,0:T(8,128)}, f32[8,512]{1,0:T(8,128)}) custom-call(f32[512,4096]{1,0:T(8,128)S(1)} %get-tuple-element.12.m_ref, f32[8,512]{1,0:T(8,128)S(1)} %get-tuple-element.13.u_ref, f32[8,4096]{1,0:T(8,128)S(1)} %get-tuple-element.14.c_ref, ...), custom_call_target="tpu_custom_call" | custom-call | tf_op jit(solution)/shard_map/pallas_call | solution.py:526

commit v3 on v2

--- a/solution.py
+++ b/solution.py
@@ -14,9 +14,13 @@
 EPSILON = 1e-06
 TILE = 512
 PARTS = 4
+SLOTS = (0, -1, 1, 2, -2, 3, -3, 4)
 XS, YS, CORES = 4, 4, 2
 PLANE = XS * CORES
 DP = YS * PLANE
+OFFSETS = sorted(
+    ((dy, dx, dc) for dy in range(YS) for dx in range(XS) for dc in range(CORES)),
+    key=lambda o: (-min(o[0], YS - o[0]) - min(o[1], XS - o[1]), -o[2]))
 
 
 def nn(a, b):
@@ -75,8 +79,8 @@
     sign = (1, -1)
     a_to = [y * PLANE + lax.rem(xc + k, PLANE) for k in range(PLANE)]
     b_to = [lax.rem(y + k, YS) * PLANE + xc for k in range(YS)]
-    d_to = [lax.rem(dp + k, DP) for k in range(DP)]
-    chips = [lax.rem(chip + k, XS * YS) for k in range(XS * YS)]
+    d_to = [lax.rem(y + dy, YS) * PLANE + lax.rem(xq + dx, XS) * CORES + lax.rem(core + dc, CORES) for dy, dx, dc in OFFSETS]
+    chips = [lax.rem(y + dy, YS) * XS + lax.rem(xq + dx, XS) for dy, dx, dc in OFFSETS if dc == 0]
     p_to = [c * CORES + core for c in chips]
     partner = chip * CORES + (1 - core)
 
@@ -91,18 +95,20 @@
     own_rows = own_cols
     chip_cols = pl.ds(pl.multiple_of(chip * 256, 256), 256)
     lx = pltpu.make_async_copy(x_hbm, x_ref, lsem.at[0])
-    lw = pltpu.make_async_copy(w_hbm.at[:, chip_cols], wp.at[own_rows, :], lsem.at[1])
+    lw = [pltpu.make_async_copy(
+        w_hbm.at[:, pl.ds(pl.multiple_of(chip * 256 + c * 128, 128), 128)], wp.at[c, own_rows], lsem.at[1 + 5 * c])
+        for c in range(CORES)]
     le = pltpu.make_async_copy(e_hbm, e_ref, lsem.at[2])
     lg = pltpu.make_async_copy(g_hbm, gbuf.at[own], lsem.at[3])
     lc = pltpu.make_async_copy(wc_hbm, wc_ref, lsem.at[5])
     lp = pltpu.make_async_copy(g_hbm, gpad.at[pl.ds(pl.multiple_of(lax.rem(me, 4) * 32, 32), 32)], lsem.at[4])
-    for c in (lc, lx, lg, le, lw):
+    for c in (lc, lx, lg, le, *lw):
         c.start()
 
     barrier = pltpu.get_barrier_semaphore()
     for z in z_all[1:]:
         pl.semaphore_signal(barrier, inc=1, device_id={"tensor": z}, device_id_type=MESH)
-    for d in d_to[1:]:
+    for d in d_to[:-1]:
         pl.semaphore_signal(barrier, inc=1, device_id={"dp": d}, device_id_type=MESH)
     gpad[...] = jnp.zeros_like(gpad)
     lp.start()
@@ -114,27 +120,25 @@
     def steps(d, h):
         return 4 if d == h else 3
 
-    def ring_copy(buf, rows, part, cols, send, recv, d, h, s):
+    def ring_copy(buf, rows, part, send, recv, d, h, s):
         block = lax.rem(me - sign[d] * s + n, n)
         at = pl.ds(pl.multiple_of(block * rows + h * part, part), part)
         return pltpu.make_async_remote_copy(
-            src_ref=buf.at[at, cols], dst_ref=buf.at[at, cols],
+            src_ref=buf.at[at], dst_ref=buf.at[at],
             send_sem=send, recv_sem=recv.at[d, h, s],
             device_id={"tensor": z_to[d]}, device_id_type=MESH)
 
     def g_copy(d, h, s):
-        return ring_copy(gbuf, 32, 16, slice(None), g_send, g_recv, d, h, s)
-
-    core_cols = pl.ds(pl.multiple_of(core * 128, 128), 128)
+        return ring_copy(gbuf, 32, 16, g_send, g_recv, d, h, s)
 
     def w_copy(d, h, s):
-        return ring_copy(wp, 512, 256, core_cols, w_send, w_recv, d, h, s)
+        return ring_copy(wp.at[core], 512, 256, w_send, w_recv, d, h, s)
 
     def wc_copy(d, h, s):
         block = lax.rem(me - sign[d] * (s + 1) + n, n)
         at = pl.ds(pl.multiple_of(block * 512 + h * 256, 256), 256)
         return pltpu.make_async_remote_copy(
-            src_ref=wp.at[at, core_cols], dst_ref=wp.at[at, core_cols],
+            src_ref=wp.at[core, at], dst_ref=wp.at[core, at],
             send_sem=wc_send, recv_sem=wc_recv.at[s],
             device_id={"dp": partner}, device_id_type=MESH)
 
@@ -156,12 +160,16 @@
                 if s > 0 and s - 1 < steps(d, h):
                     wc_copy(d, h, s - 1).start()
 
+    def slot_cols(shift):
+        return pl.ds(SLOTS.index(shift) * 512, 512)
+
     def xz_copy(k):
-        src = pl.ds(pl.multiple_of(z_all[k] * 32, 32), 32)
-        return pltpu.make_async_remote_copy(
-            src_ref=x_ref.at[src], dst_ref=xa.at[mine, own_cols],
-            send_sem=xz_send, recv_sem=xz_recv,
-            device_id={"tensor": z_all[k]}, device_id_type=MESH)
+        src = pl.ds(pl.multiple_of(lax.rem(me + k + n, n) * 32, 32), 32)
+        there = 4 if k == 4 else -k
+        return pltpu.make_async_remote_copy(
+            src_ref=x_ref.at[src], dst_ref=xa.at[mine, slot_cols(there)],
+            send_sem=xz_send, recv_sem=xz_recv.at[SLOTS.index(there) // 4],
+            device_id={"tensor": lax.rem(me + k + n, n)}, device_id_type=MESH)
 
     shifts = (0, -1, 1, 2)
 
@@ -178,8 +186,8 @@
         else:
             rx, ry = rb, ra
         block = lax.rem(y + ry + YS, YS) * XS + lax.rem(xq + rx + XS, XS)
-        at = pl.ds(pl.multiple_of(block * 32 + h * 16, 16), 16)
-        cols = (slice(None), slice(None), pl.ds(0, 2048), pl.ds(2048, 2048))[kind]
+        at = pl.ds(pl.multiple_of(block * 32 + (16 if kind == 3 else 0), 16), 32 if kind < 2 else 16)
+        cols = pl.ds(h * 2048, 2048)
         return pltpu.make_async_remote_copy(
             src_ref=xa.at[at, cols], dst_ref=xa.at[at, cols],
             send_sem=xy_send, recv_sem=xy_recv.at[h, stage, min(kind, 2)],
@@ -192,15 +200,11 @@
     def xy_one(h, stage):
         xy_copy(h, stage, 0).wait_recv()
         xy_copy(h, stage, 2).start()
-        if stage == 0:
-            xy_full(h, 2)
         xy_copy(h, stage, 1).wait_recv()
         xy_copy(h, stage, 3).start()
-        if stage == 0:
-            xy_full(h, 3)
 
     def xy_two(h, stage):
-        settle(xa.at[pl.ds(0, 16)], xy_recv.at[h, stage, 2])
+        settle(xa.at[pl.ds(0, 32), pl.ds(0, 2048)], xy_recv.at[h, stage, 2])
         if stage == 0:
             xy_full(h, 4)
 
@@ -252,21 +256,64 @@
             src_ref=src, dst_ref=dst, send_sem=send.at[1], recv_sem=recv.at[1],
             device_id={"dp": b_to[k]}, device_id_type=MESH)
 
+    def merge(low, high):
+        @pl.loop(low, high, step=TILE)
+        def _(c):
+            cols = pl.ds(pl.multiple_of(c, TILE), TILE)
+            merged_ref[:, cols] = e_ref[:, cols].astype(F32) + nn(xt_ref[...], gbuf[:, cols])
+
+    def product(shift, first=False):
+        t = lax.rem(me + shift + n, n)
+        at = pl.ds(pl.multiple_of(t * 512, 512), 512)
+
+        @pl.loop(0, 512, step=256)
+        def _(r):
+            rows = pl.ds(pl.multiple_of(r, 256), 256)
+            strips = jnp.concatenate([wp[0, at], wp[1, at]], axis=1)
+            part = nn(xa[rows, slot_cols(shift)], strips)
+            yacc[rows, :] = part if first else yacc[rows, :] + part
+
+    def w_ready(s):
+        settle(wp.at[0, pl.ds(0, 1024 if s < 3 else 512)], wc_recv.at[s])
+
+    def piece(j):
+        return pl.ds(pl.multiple_of(j * 128, 128), 128)
+
+    my_piece = piece(dp)
+
+    def r_copy(to):
+        return pltpu.make_async_remote_copy(
+            src_ref=cbuf.at[:, piece(to)], dst_ref=cin.at[dp],
+            send_sem=cf_send.at[0], recv_sem=cf_recv.at[0],
+            device_id={"dp": to}, device_id_type=MESH)
+
+    def s_copy(k):
+        return pltpu.make_async_remote_copy(
+            src_ref=coef_ref.at[:, my_piece], dst_ref=coef_ref.at[:, my_piece],
+            send_sem=cf_send.at[1], recv_sem=cf_recv.at[1],
+            device_id={"dp": d_to[k]}, device_id_type=MESH)
+
     lc.wait()
     for k in range(1, n):
         c_copy(k).start()
     wz[core, y, xq, pl.ds(pl.multiple_of(me * 8, 8), 8)] = wc_ref[:, pl.ds(pl.multiple_of(dp * 128, 128), 128)]
     lx.wait()
+    for k in (1, -1, -2, 2, -3, 3, 4):
+        xz_copy(k).start()
     lg.wait()
-    xa[mine, own_cols] = x_ref[own, :]
+    g_step(0)
+    for c in lw:
+        c.wait()
+    w_step(0)
+    xa[mine, slot_cols(0)] = x_ref[own, :]
     xt_ref[...] = x_ref[...].T
     settle(wz.at[0, 0, 0, pl.ds(0, 56)], c_recv)
     for h in range(2):
         for k in range(1, 4):
             p_copy(h, 0, k).start()
-    for k in range(1, n):
-        xz_copy(k).start()
-    g_step(0)
+    settle(xa.at[pl.ds(0, 32), pl.ds(0, 1536)], xz_recv.at[0])
+    xy_full(0, 0)
+    xy_full(0, 1)
     le.wait()
     se_ref[...] = jnp.zeros_like(se_ref)
 
@@ -281,7 +328,14 @@
         settle(wz.at[0, 0, pl.ds(0, 3), pl.ds(0, 32)], p_recv.at[h, 0])
         for k in range(1, 4):
             p_copy(h, 1, k).start()
+    settle(xa.at[pl.ds(0, 32), pl.ds(0, 2048)], xz_recv.at[1])
+    xy_full(1, 0)
+    xy_full(1, 1)
+    xy_one(0, 0)
+    xy_full(0, 2)
+    xy_one(0, 1)
     sketch_error(2048, 4096)
+    g_step(1)
     for h in range(2):
         settle(wz.at[0, pl.ds(0, 3), :, pl.ds(0, 32)], p_recv.at[h, 1])
         k_copy(h).start()
@@ -296,12 +350,13 @@
     for k in range(1, n):
         t_copy(k).start()
     tdst[me] = tsrc[me]
-    settle(xa.at[pl.ds(0, 32), pl.ds(0, 3584)], xz_recv)
-    for h in range(2):
-        xy_full(h, 0)
-    for h in range(2):
-        xy_full(h, 1)
-    g_step(1)
+    xy_one(1, 0)
+    xy_full(1, 2)
+    xy_full(0, 3)
+    xy_full(1, 3)
+    w_step(1)
+    xy_two(0, 0)
+    xy_one(1, 1)
     settle(tdst.at[pl.ds(0, 7)], t_recv)
     tokens = jnp.concatenate(
         [tdst[0] + tdst[1] + tdst[2] + tdst[3], tdst[4] + tdst[5] + tdst[6] + tdst[7]], axis=1)
@@ -311,11 +366,10 @@
     for k in ks_a:
         a_copy(k, sk_src.at[0], abuf.at[xc], sk_send, sk_recv).start()
     abuf[xc] = sketch
-    for h in range(2):
-        xy_one(h, 0)
-    for h in range(2):
-        xy_one(h, 1)
     g_step(2)
+    xy_two(1, 0)
+    xy_one(0, 2)
+    xy_one(1, 2)
     settle(abuf.at[pl.ds(0, PLANE - 1)], sk_recv.at[0])
     total = abuf[0]
     for k in range(1, PLANE):
@@ -324,13 +378,12 @@
     for k in ks_b:
         b_copy(k, sk_src.at[1], bbuf.at[y], sk_send, sk_recv).start()
     bbuf[y] = total
-    for h in range(2):
-        xy_two(h, 0)
-    for h in range(2):
-        xy_two(h, 1)
+    w_step(2)
+    xy_one(0, 3)
+    xy_one(1, 3)
     g_step(3)
-    lw.wait()
-    w_step(0)
+    xy_one(0, 4)
+    xy_one(1, 4)
     settle(bbuf.at[pl.ds(0, YS - 1)], sk_recv.at[1])
     total = bbuf[0]
     for k in range(1, YS):
@@ -345,79 +398,34 @@
         cols = pl.ds(pl.multiple_of(c, TILE), TILE)
         cbuf[:, cols] = sum3(nn(u3, e_ref[:, cols]))
 
+    w_step(3)
     for h in range(2):
-        xy_one(h, 2)
-    for h in range(2):
-        xy_one(h, 3)
-    g_step(4)
-
-    @pl.loop(0, 4096, step=TILE)
-    def _(c):
-        cols = pl.ds(pl.multiple_of(c, TILE), TILE)
-        cbuf[:, cols] += sum3(nn(v3, gbuf[:, cols]))
-
-    def piece(j):
-        return pl.ds(pl.multiple_of(j * 128, 128), 128)
-
-    my_piece = piece(dp)
-
-    def r_copy(k):
-        return pltpu.make_async_remote_copy(
-            src_ref=cbuf.at[:, piece(d_to[k])], dst_ref=cin.at[dp],
-            send_sem=cf_send.at[0], recv_sem=cf_recv.at[0],
-            device_id={"dp": d_to[k]}, device_id_type=MESH)
-
-    def s_copy(k):
-        return pltpu.make_async_remote_copy(
-            src_ref=coef_ref.at[:, my_piece], dst_ref=coef_ref.at[:, my_piece],
-            send_sem=cf_send.at[1], recv_sem=cf_recv.at[1],
-            device_id={"dp": d_to[k]}, device_id_type=MESH)
-
-    for k in range(1, DP):
-        r_copy(k).start()
-    cin[dp] = cbuf[:, my_piece]
-    w_step(1)
-    for h in range(2):
-        xy_one(h, 4)
-
-    def merge(low, high):
-        @pl.loop(low, high, step=TILE)
-        def _(c):
-            cols = pl.ds(pl.multiple_of(c, TILE), TILE)
-            merged_ref[:, cols] = e_ref[:, cols].astype(F32) + nn(xt_ref[...], gbuf[:, cols])
-
-    def product(shift, first=False):
-        t = lax.rem(me + shift + n, n)
-        at = pl.ds(pl.multiple_of(t * 512, 512), 512)
-
-        @pl.loop(0, 512, step=256)
-        def _(r):
-            rows = pl.ds(pl.multiple_of(r, 256), 256)
-            part = nn(xa[rows, at], wp[at, :])
-            yacc[rows, :] = part if first else yacc[rows, :] + part
-
-    def w_ready(s):
-        settle(wp.at[pl.ds(0, 1024 if s < 3 else 512), pl.ds(0, 128)], wc_recv.at[s])
-
-    merge(0, 2048)
-    w_step(2)
-    settle(cin.at[pl.ds(0, DP - 1)], cf_recv.at[0])
-    total = cin[0]
-    for k in range(1, DP):
-        total += cin[k]
-    coef_ref[:, my_piece] = total * (1.0 / 32)
-    for k in range(1, DP):
-        s_copy(k).start()
-    merge(2048, 4096)
-    for h in range(2):
-        for stage in range(2, 5):
+        for stage in range(1, 5):
             xy_two(h, stage)
     product(0, True)
-    w_step(3)
-    for s in range(2):
-        w_ready(s)
-        product(s + 1)
-        product(-s - 1)
+    w_ready(0)
+    product(1)
+    product(-1)
+    w_ready(1)
+    product(2)
+    product(-2)
+    g_step(4)
+
+    def coefficients(row):
+        @pl.loop(0, 1024, step=TILE)
+        def _(c):
+            cols = pl.ds(pl.multiple_of(row * 1024 + c, TILE), TILE)
+            cbuf[:, cols] += sum3(nn(v3, gbuf[:, cols]))
+
+    for dy in (2, 1, 3):
+        row = lax.rem(y + dy, YS)
+        coefficients(row)
+        for j in range(PLANE):
+            r_copy(row * PLANE + j).start()
+    coefficients(y)
+    for k in ks_a:
+        r_copy(a_to[k]).start()
+    cin[dp] = cbuf[:, my_piece]
     w_step(4)
     w_ready(2)
     product(3)
@@ -425,9 +433,17 @@
     w_ready(3)
     product(4)
     yb[...] = yacc[...].astype(BF16)
-    for k in range(1, XS * YS):
+    for k in range(XS * YS - 1):
         y_copy(k).start()
     out_ref[:, chip_cols] = yb[mine, :]
+    settle(cin.at[pl.ds(0, DP - 1)], cf_recv.at[0])
+    total = cin[0]
+    for k in range(1, DP):
+        total += cin[k]
+    coef_ref[:, my_piece] = total * (1.0 / 32)
+    for k in range(DP - 1):
+        s_copy(k).start()
+    merge(0, 4096)
     settle(coef_ref.at[:, pl.ds(0, 128 * (DP - 1))], cf_recv.at[1])
     settle(cbuf.at[:, pl.ds(0, 128 * (DP - 1))], cf_send.at[0])
     settle(coef_ref.at[:, pl.ds(0, 128 * (DP - 1))], cf_send.at[1])
@@ -441,8 +457,8 @@
         settle(wz.at[0, 0, pl.ds(0, 3), pl.ds(0, 32)], p_send.at[h, 0])
         settle(wz.at[0, pl.ds(0, 3), :, pl.ds(0, 32)], p_send.at[h, 1])
     settle(gbuf.at[pl.ds(0, 224)], g_send)
-    settle(wp.at[pl.ds(0, 3584), pl.ds(0, 128)], w_send)
-    settle(wp.at[pl.ds(0, 3584), pl.ds(0, 128)], wc_send)
+    settle(wp.at[0, pl.ds(0, 3584)], w_send)
+    settle(wp.at[0, pl.ds(0, 3584)], wc_send)
     settle(xa.at[pl.ds(0, 480)], xy_send)
     settle(yb.at[pl.ds(0, 480)], y_recv)
     settle(yb.at[pl.ds(0, 480)], y_send)
@@ -490,7 +506,7 @@
             VM((512, 4096), BF16),
             VM((256, 4096), BF16),
             VM((512, 4096), BF16),
-            VM((4096, 256), BF16),
+            VM((CORES, 4096, 128), BF16),
             VM((512, 256), F32),
             VM((512, 256), BF16),
             VM((8, 4096), F32),
@@ -506,9 +522,9 @@
             VM((YS, 8, 512), F32),
             VM((DP, 8, 128), F32),
             VM((2, 8, 512), F32),
-            D((6,)),
+            D((7,)),
             D, D((2, 2, 4)),
-            D, D,
+            D, D((2,)),
             D, D((2, 5, 3)),
             D, D((2, 2, 4)),
             D, D((4,)),

time: 74.3 us -> 64.6 us (0.87)
  Pallas kernels: 73.5 us -> 63.9 us
    pallas_call x1, Pallas kernels: 70.9 us -> 61.2 us  [shards(): pl.pallas_call(main_kernel, out_shape=(VM((32, 4096), BF16), VM((8, 4096)...]
where the time goes in v3:
time: 64.6 us
  Pallas kernels  63.9 us (99%)
    pallas_call x1, Pallas kernels, shards(): pl.pallas_call(main_kernel, out_shape=(VM((32, 4096), BF16), VM((8, 4096)...  61.2 us
    pallas_call x1, Pallas kernels, shards(): pl.pallas_call(error_kernel, out_shape=(S((512, 4096), BF16), S((32, 4096...  2.68 us

profile of v3, /device:TPU:1, one launch (start us, length us, event | category | flops | bytes accessed | tf_op | source)
XLA Modules:
  0.0 64.6 jit_solution(16360913272789356534)
XLA Ops:
  0.6 61.2 %shard_map.84 = (bf16[32,4096]{1,0:T(8,128)(2,1)S(1)}, f32[8,4096]{1,0:T(8,128)S(1)}, f32[512,4096]{1,0:T(8,128)S(1)}, f32[8,512]{1,0:T(8,128)S(1)}) custom-call(bf16[256,512]{1,0:T(8,128)(2,1)} %x_hbm.1, bf16[512,4096]{1,0:T(8,128)(2,1)} %w_hbm.1, bf16[32,4096]{1,0:T(8,128)(2,1)} %g_hbm.1, bf16[512,4096]{1,0:T(8,128)(2,1)} %bitcast.4, f32[8,4096]{1,0:T(8,128)} %bitcast.5), custom_call_target="tpu_custom_call" | custom-call | tf_op jit(solution)/shard_map/pallas_call | solution.py:499
  61.9 2.7 %shard_map.85 = (bf16[512,4096]{1,0:T(8,128)(2,1)}, bf16[32,4096]{1,0:T(8,128)(2,1)}, f32[8,4096]{1,0:T(8,128)}, f32[8,512]{1,0:T(8,128)}) custom-call(f32[512,4096]{1,0:T(8,128)S(1)} %get-tuple-element.12.m_ref, f32[8,512]{1,0:T(8,128)S(1)} %get-tuple-element.13.u_ref, f32[8,4096]{1,0:T(8,128)S(1)} %get-tuple-element.14.c_ref, ...), custom_call_target="tpu_custom_call" | custom-call | tf_op jit(solution)/shard_map/pallas_call | solution.py:542

commit v4 on v3

--- a/solution.py
+++ b/solution.py
@@ -13,7 +13,7 @@
 BF16 = jnp.bfloat16
 EPSILON = 1e-06
 TILE = 512
-PARTS = 4
+PARTS = 8
 SLOTS = (0, -1, 1, 2, -2, 3, -3, 4)
 XS, YS, CORES = 4, 4, 2
 PLANE = XS * CORES
@@ -190,7 +190,7 @@
         cols = pl.ds(h * 2048, 2048)
         return pltpu.make_async_remote_copy(
             src_ref=xa.at[at, cols], dst_ref=xa.at[at, cols],
-            send_sem=xy_send, recv_sem=xy_recv.at[h, stage, min(kind, 2)],
+            send_sem=xy_send, recv_sem=xy_recv.at[h, stage, kind // 2],
             device_id={"dp": shifted(axis, go) * CORES + core}, device_id_type=MESH)
 
     def xy_full(h, stage):
@@ -198,13 +198,12 @@
         xy_copy(h, stage, 1).start()
 
     def xy_one(h, stage):
-        xy_copy(h, stage, 0).wait_recv()
+        settle(xa.at[pl.ds(0, 64), pl.ds(0, 2048)], xy_recv.at[h, stage, 0])
         xy_copy(h, stage, 2).start()
-        xy_copy(h, stage, 1).wait_recv()
         xy_copy(h, stage, 3).start()
 
     def xy_two(h, stage):
-        settle(xa.at[pl.ds(0, 32), pl.ds(0, 2048)], xy_recv.at[h, stage, 2])
+        settle(xa.at[pl.ds(0, 32), pl.ds(0, 2048)], xy_recv.at[h, stage, 1])
         if stage == 0:
             xy_full(h, 4)
 
@@ -238,7 +237,7 @@
     def k_copy(h):
         at = wz.at[core, :, :, pl.ds(h * 32, 32)]
         return pltpu.make_async_remote_copy(
-            src_ref=at, dst_ref=at, send_sem=k_send.at[h], recv_sem=k_recv.at[h],
+            src_ref=at, dst_ref=at, send_sem=k_send, recv_sem=k_recv,
             device_id={"dp": partner}, device_id_type=MESH)
 
     def t_copy(k):
@@ -262,16 +261,13 @@
             cols = pl.ds(pl.multiple_of(c, TILE), TILE)
             merged_ref[:, cols] = e_ref[:, cols].astype(F32) + nn(xt_ref[...], gbuf[:, cols])
 
-    def product(shift, first=False):
+    def term(shift):
         t = lax.rem(me + shift + n, n)
         at = pl.ds(pl.multiple_of(t * 512, 512), 512)
-
-        @pl.loop(0, 512, step=256)
-        def _(r):
-            rows = pl.ds(pl.multiple_of(r, 256), 256)
-            strips = jnp.concatenate([wp[0, at], wp[1, at]], axis=1)
-            part = nn(xa[rows, slot_cols(shift)], strips)
-            yacc[rows, :] = part if first else yacc[rows, :] + part
+        return nn(xa[:, slot_cols(shift)], jnp.concatenate([wp[0, at], wp[1, at]], axis=1))
+
+    def product(*shifts):
+        yacc[...] += sum(term(shift) for shift in shifts)
 
     def w_ready(s):
         settle(wp.at[0, pl.ds(0, 1024 if s < 3 else 512)], wc_recv.at[s])
@@ -339,8 +335,7 @@
     for h in range(2):
         settle(wz.at[0, pl.ds(0, 3), :, pl.ds(0, 32)], p_recv.at[h, 1])
         k_copy(h).start()
-    for h in range(2):
-        k_copy(h).wait_recv()
+    settle(wz.at[0], k_recv)
     for d in range(DP):
         w3_ref[:, d * 128 : d * 128 + 128] = split3(wz[d % CORES, d // PLANE, d % PLANE // CORES])
     lp.wait()
@@ -357,6 +352,7 @@
     w_step(1)
     xy_two(0, 0)
     xy_one(1, 1)
+    g_step(2)
     settle(tdst.at[pl.ds(0, 7)], t_recv)
     tokens = jnp.concatenate(
         [tdst[0] + tdst[1] + tdst[2] + tdst[3], tdst[4] + tdst[5] + tdst[6] + tdst[7]], axis=1)
@@ -366,7 +362,6 @@
     for k in ks_a:
         a_copy(k, sk_src.at[0], abuf.at[xc], sk_send, sk_recv).start()
     abuf[xc] = sketch
-    g_step(2)
     xy_two(1, 0)
     xy_one(0, 2)
     xy_one(1, 2)
@@ -402,13 +397,11 @@
     for h in range(2):
         for stage in range(1, 5):
             xy_two(h, stage)
-    product(0, True)
+    yacc[...] = term(0)
     w_ready(0)
-    product(1)
-    product(-1)
+    product(1, -1)
     w_ready(1)
-    product(2)
-    product(-2)
+    product(2, -2)
     g_step(4)
 
     def coefficients(row):
@@ -428,11 +421,9 @@
     cin[dp] = cbuf[:, my_piece]
     w_step(4)
     w_ready(2)
-    product(3)
-    product(-3)
+    product(3, -3)
     w_ready(3)
-    product(4)
-    yb[...] = yacc[...].astype(BF16)
+    yb[...] = (yacc[...] + term(4)).astype(BF16)
     for k in range(XS * YS - 1):
         y_copy(k).start()
     out_ref[:, chip_cols] = yb[mine, :]
@@ -452,8 +443,8 @@
     settle(xa.at[pl.ds(0, 32), pl.ds(0, 3584)], xz_send)
     settle(wz.at[0, 0, 0, pl.ds(0, 56)], c_send)
     settle(tdst.at[pl.ds(0, 7)], t_send)
+    settle(wz.at[0], k_send)
     for h in range(2):
-        k_copy(h).wait_send()
         settle(wz.at[0, 0, pl.ds(0, 3), pl.ds(0, 32)], p_send.at[h, 0])
         settle(wz.at[0, pl.ds(0, 3), :, pl.ds(0, 32)], p_send.at[h, 1])
     settle(gbuf.at[pl.ds(0, 224)], g_send)
@@ -525,7 +516,7 @@
             D((7,)),
             D, D((2, 2, 4)),
             D, D((2,)),
-            D, D((2, 5, 3)),
+            D, D((2, 5, 2)),
             D, D((2, 2, 4)),
             D, D((4,)),
             D, D,
@@ -533,7 +524,7 @@
             D((2,)), D((2,)),
             D, D,
             D((2, 2)), D((2, 2)),
-            D((2,)), D((2,)),
+            D, D,
             D, D,
         ],
         compiler_params=pltpu.CompilerParams(

time: 64.6 us -> 63.8 us (0.988)
  Pallas kernels: 63.9 us -> 63.1 us
where the time goes in v4:
time: 63.8 us; the launch traced here: 63.7 us
  Pallas kernels  63.1 us (99%)
  between operations  0.64 us (1%)
    pallas_call x1, Pallas kernels, shards(): pl.pallas_call(main_kernel, out_shape=(VM((32, 4096), BF16), VM((8, 4096)...  60.6 us
    pallas_call x1, Pallas kernels, shards(): pl.pallas_call(error_kernel, out_shape=(S((512, 4096), BF16), S((32, 4096...  2.46 us

profile of v4, /device:TPU:1, one launch (start us, length us, event | category | flops | bytes accessed | tf_op | source)
XLA Modules:
  0.0 63.7 jit_solution(15844077724695296731)
XLA Ops:
  0.6 60.6 %shard_map.84 = (bf16[32,4096]{1,0:T(8,128)(2,1)S(1)}, f32[8,4096]{1,0:T(8,128)S(1)}, f32[512,4096]{1,0:T(8,128)S(1)}, f32[8,512]{1,0:T(8,128)S(1)}) custom-call(bf16[256,512]{1,0:T(8,128)(2,1)} %x_hbm.1, bf16[512,4096]{1,0:T(8,128)(2,1)} %w_hbm.1, bf16[32,4096]{1,0:T(8,128)(2,1)} %g_hbm.1, bf16[512,4096]{1,0:T(8,128)(2,1)} %bitcast.4, f32[8,4096]{1,0:T(8,128)} %bitcast.5), custom_call_target="tpu_custom_call" | custom-call | tf_op jit(solution)/shard_map/pallas_call | solution.py:490
  61.3 2.5 %shard_map.85 = (bf16[512,4096]{1,0:T(8,128)(2,1)}, bf16[32,4096]{1,0:T(8,128)(2,1)}, f32[8,4096]{1,0:T(8,128)}, f32[8,512]{1,0:T(8,128)}) custom-call(f32[512,4096]{1,0:T(8,128)S(1)} %get-tuple-element.12.m_ref, f32[8,512]{1,0:T(8,128)S(1)} %get-tuple-element.13.u_ref, f32[8,4096]{1,0:T(8,128)S(1)} %get-tuple-element.14.c_ref, ...), custom_call_target="tpu_custom_call" | custom-call | tf_op jit(solution)/shard_map/pallas_call | solution.py:533

commit v5 on v4

--- a/solution.py
+++ b/solution.py
@@ -108,11 +108,12 @@
     barrier = pltpu.get_barrier_semaphore()
     for z in z_all[1:]:
         pl.semaphore_signal(barrier, inc=1, device_id={"tensor": z}, device_id_type=MESH)
-    for d in d_to[:-1]:
+    near = [y * PLANE + lax.rem(xq + k, XS) * CORES + core for k in range(1, XS)] + b_to[1:] + [partner]
+    for d in near:
         pl.semaphore_signal(barrier, inc=1, device_id={"dp": d}, device_id_type=MESH)
     gpad[...] = jnp.zeros_like(gpad)
     lp.start()
-    pl.semaphore_wait(barrier, 7 + 31)
+    pl.semaphore_wait(barrier, 7 + 3 + 3 + 1)
 
     def settle(ref, sem):
         pltpu.make_async_copy(ref, ref, sem).wait()
@@ -365,6 +366,7 @@
     xy_two(1, 0)
     xy_one(0, 2)
     xy_one(1, 2)
+    w_step(2)
     settle(abuf.at[pl.ds(0, PLANE - 1)], sk_recv.at[0])
     total = abuf[0]
     for k in range(1, PLANE):
@@ -373,10 +375,9 @@
     for k in ks_b:
         b_copy(k, sk_src.at[1], bbuf.at[y], sk_send, sk_recv).start()
     bbuf[y] = total
-    w_step(2)
+    g_step(3)
     xy_one(0, 3)
     xy_one(1, 3)
-    g_step(3)
     xy_one(0, 4)
     xy_one(1, 4)
     settle(bbuf.at[pl.ds(0, YS - 1)], sk_recv.at[1])
@@ -387,21 +388,13 @@
     u_ref[...] = unit
     u3 = split3(unit)
     v3 = split3(sum3(nt(u3, x_ref[...])))
+    w_step(3)
 
     @pl.loop(0, 4096, step=TILE)
     def _(c):
         cols = pl.ds(pl.multiple_of(c, TILE), TILE)
         cbuf[:, cols] = sum3(nn(u3, e_ref[:, cols]))
 
-    w_step(3)
-    for h in range(2):
-        for stage in range(1, 5):
-            xy_two(h, stage)
-    yacc[...] = term(0)
-    w_ready(0)
-    product(1, -1)
-    w_ready(1)
-    product(2, -2)
     g_step(4)
 
     def coefficients(row):
@@ -420,6 +413,14 @@
         r_copy(a_to[k]).start()
     cin[dp] = cbuf[:, my_piece]
     w_step(4)
+    for h in range(2):
+        for stage in range(1, 5):
+            xy_two(h, stage)
+    yacc[...] = term(0)
+    w_ready(0)
+    product(1, -1)
+    w_ready(1)
+    product(2, -2)
     w_ready(2)
     product(3, -3)
     w_ready(3)

time: 63.8 us -> 62.9 us (0.986)
  Pallas kernels: 63.1 us -> 62.2 us
    pallas_call x1, Pallas kernels: 60.6 us -> 59.7 us  [shards(): pl.pallas_call(main_kernel, out_shape=(VM((32, 4096), BF16), VM((8, 4096)...]
where the time goes in v5:
time: 62.9 us; the launch traced here: 62.8 us
  Pallas kernels  62.2 us (99%)
  between operations  0.64 us (1%)
    pallas_call x1, Pallas kernels, shards(): pl.pallas_call(main_kernel, out_shape=(VM((32, 4096), BF16), VM((8, 4096)...  59.7 us
    pallas_call x1, Pallas kernels, shards(): pl.pallas_call(error_kernel, out_shape=(S((512, 4096), BF16), S((32, 4096...  2.46 us

profile of v5, /device:TPU:1, one launch (start us, length us, event | category | flops | bytes accessed | tf_op | source)
XLA Modules:
  0.0 62.8 jit_solution(15569360884394413192)
XLA Ops:
  0.6 59.7 %shard_map.84 = (bf16[32,4096]{1,0:T(8,128)(2,1)S(1)}, f32[8,4096]{1,0:T(8,128)S(1)}, f32[512,4096]{1,0:T(8,128)S(1)}, f32[8,512]{1,0:T(8,128)S(1)}) custom-call(bf16[256,512]{1,0:T(8,128)(2,1)} %x_hbm.1, bf16[512,4096]{1,0:T(8,128)(2,1)} %w_hbm.1, bf16[32,4096]{1,0:T(8,128)(2,1)} %g_hbm.1, bf16[512,4096]{1,0:T(8,128)(2,1)} %bitcast.4, f32[8,4096]{1,0:T(8,128)} %bitcast.5), custom_call_target="tpu_custom_call" | custom-call | tf_op jit(solution)/shard_map/pallas_call | solution.py:491
  60.4 2.5 %shard_map.85 = (bf16[512,4096]{1,0:T(8,128)(2,1)}, bf16[32,4096]{1,0:T(8,128)(2,1)}, f32[8,4096]{1,0:T(8,128)}, f32[8,512]{1,0:T(8,128)}) custom-call(f32[512,4096]{1,0:T(8,128)S(1)} %get-tuple-element.12.m_ref, f32[8,512]{1,0:T(8,128)S(1)} %get-tuple-element.13.u_ref, f32[8,4096]{1,0:T(8,128)S(1)} %get-tuple-element.14.c_ref, ...), custom_call_target="tpu_custom_call" | custom-call | tf_op jit(solution)/shard_map/pallas_call | solution.py:534

commit v6 on v5

--- a/solution.py
+++ b/solution.py
@@ -61,7 +61,7 @@
 def main_kernel(
     x_hbm, w_hbm, g_hbm, e_hbm, wc_hbm,
     out_ref, coef_ref, merged_ref, u_ref,
-    x_ref, e_ref, gbuf, xa, wp, yacc, yb, wc_ref, wz, w3_ref, gpad, tsrc, tdst, se_ref, xt_ref, cbuf,
+    x_ref, e_ref, gbuf, xa, wp, yacc, yb, wc_ref, wz, w3_ref, gpad, tsrc, tdst, se_ref, xt_ref, xg_ref, cbuf,
     abuf, bbuf, cin, sk_src,
     lsem, g_send, g_recv, xz_send, xz_recv, xy_send, xy_recv, w_send, w_recv, wc_send, wc_recv,
     y_send, y_recv, sk_send, sk_recv, cf_send, cf_recv, c_send, c_recv, p_send, p_recv, k_send, k_recv,
@@ -99,7 +99,7 @@
         w_hbm.at[:, pl.ds(pl.multiple_of(chip * 256 + c * 128, 128), 128)], wp.at[c, own_rows], lsem.at[1 + 5 * c])
         for c in range(CORES)]
     le = pltpu.make_async_copy(e_hbm, e_ref, lsem.at[2])
-    lg = pltpu.make_async_copy(g_hbm, gbuf.at[own], lsem.at[3])
+    lg = pltpu.make_async_copy(g_hbm, gbuf.at[pl.ds(0, 32)], lsem.at[3])
     lc = pltpu.make_async_copy(wc_hbm, wc_ref, lsem.at[5])
     lp = pltpu.make_async_copy(g_hbm, gpad.at[pl.ds(pl.multiple_of(lax.rem(me, 4) * 32, 32), 32)], lsem.at[4])
     for c in (lc, lx, lg, le, *lw):
@@ -130,7 +130,13 @@
             device_id={"tensor": z_to[d]}, device_id_type=MESH)
 
     def g_copy(d, h, s):
-        return ring_copy(gbuf, 32, 16, g_send, g_recv, d, h, s)
+        def at(shift):
+            return gbuf.at[pl.ds(SLOTS.index(4 if abs(shift) == 4 else shift) * 32 + h * 16, 16)]
+
+        return pltpu.make_async_remote_copy(
+            src_ref=at(-sign[d] * s), dst_ref=at(-sign[d] * (s + 1)),
+            send_sem=g_send, recv_sem=g_recv.at[d, h, s],
+            device_id={"tensor": z_to[d]}, device_id_type=MESH)
 
     def w_copy(d, h, s):
         return ring_copy(wp.at[core], 512, 256, w_send, w_recv, d, h, s)
@@ -303,7 +309,10 @@
         c.wait()
     w_step(0)
     xa[mine, slot_cols(0)] = x_ref[own, :]
-    xt_ref[...] = x_ref[...].T
+    for i in range(n):
+        rows = pl.ds(pl.multiple_of(lax.rem(me + SLOTS[i] + n, n) * 32, 32), 32)
+        xg_ref[i * 32 : i * 32 + 32, :] = x_ref[rows, :]
+    xt_ref[...] = xg_ref[...].T
     settle(wz.at[0, 0, 0, pl.ds(0, 56)], c_recv)
     for h in range(2):
         for k in range(1, 4):
@@ -387,21 +396,20 @@
     unit = orthonormal(total)
     u_ref[...] = unit
     u3 = split3(unit)
-    v3 = split3(sum3(nt(u3, x_ref[...])))
+    v3 = split3(sum3(nt(u3, xg_ref[0:224, :])))
+    v_last = split3(sum3(nt(u3, xg_ref[224:256, :])))
     w_step(3)
 
     @pl.loop(0, 4096, step=TILE)
     def _(c):
         cols = pl.ds(pl.multiple_of(c, TILE), TILE)
-        cbuf[:, cols] = sum3(nn(u3, e_ref[:, cols]))
+        cbuf[:, cols] = sum3(nn(u3, e_ref[:, cols]) + nn(v3, gbuf[0:224, cols]))
 
     g_step(4)
 
     def coefficients(row):
-        @pl.loop(0, 1024, step=TILE)
-        def _(c):
-            cols = pl.ds(pl.multiple_of(row * 1024 + c, TILE), TILE)
-            cbuf[:, cols] += sum3(nn(v3, gbuf[:, cols]))
+        cols = pl.ds(pl.multiple_of(row * 1024, 1024), 1024)
+        cbuf[:, cols] += sum3(nn(v_last, gbuf[224:256, cols]))
 
     for dy in (2, 1, 3):
         row = lax.rem(y + dy, YS)
@@ -509,6 +517,7 @@
             VM((8, 8, 128), F32),
             VM((24, 512), F32),
             VM((512, 256), BF16),
+            VM((256, 512), BF16),
             VM((8, 4096), F32),
             VM((PLANE, 8, 512), F32),
             VM((YS, 8, 512), F32),

time: 62.9 us -> 62.3 us (level)
  no operation moved by 1% of the time
where the time goes in v6:
time: 62.3 us; the launch traced here: 62.2 us
  Pallas kernels  61.6 us (99%)
  between operations  0.64 us (1%)
    pallas_call x1, Pallas kernels, shards(): pl.pallas_call(main_kernel, out_shape=(VM((32, 4096), BF16), VM((8, 4096)...  59.1 us
    pallas_call x1, Pallas kernels, shards(): pl.pallas_call(error_kernel, out_shape=(S((512, 4096), BF16), S((32, 4096...  2.46 us

profile of v6, /device:TPU:1, one launch (start us, length us, event | category | flops | bytes accessed | tf_op | source)
XLA Modules:
  0.0 62.2 jit_solution(13301874127267168052)
XLA Ops:
  0.6 59.1 %shard_map.84 = (bf16[32,4096]{1,0:T(8,128)(2,1)S(1)}, f32[8,4096]{1,0:T(8,128)S(1)}, f32[512,4096]{1,0:T(8,128)S(1)}, f32[8,512]{1,0:T(8,128)S(1)}) custom-call(bf16[256,512]{1,0:T(8,128)(2,1)} %x_hbm.1, bf16[512,4096]{1,0:T(8,128)(2,1)} %w_hbm.1, bf16[32,4096]{1,0:T(8,128)(2,1)} %g_hbm.1, bf16[512,4096]{1,0:T(8,128)(2,1)} %bitcast.4, f32[8,4096]{1,0:T(8,128)} %bitcast.5), custom_call_target="tpu_custom_call" | custom-call | tf_op jit(solution)/shard_map/pallas_call | solution.py:499
  59.8 2.5 %shard_map.85 = (bf16[512,4096]{1,0:T(8,128)(2,1)}, bf16[32,4096]{1,0:T(8,128)(2,1)}, f32[8,4096]{1,0:T(8,128)}, f32[8,512]{1,0:T(8,128)}) custom-call(f32[512,4096]{1,0:T(8,128)S(1)} %get-tuple-element.12.m_ref, f32[8,512]{1,0:T(8,128)S(1)} %get-tuple-element.13.u_ref, f32[8,4096]{1,0:T(8,128)S(1)} %get-tuple-element.14.c_ref, ...), custom_call_target="tpu_custom_call" | custom-call | tf_op jit(solution)/shard_map/pallas_call | solution.py:543

commit v7 on v6

--- a/solution.py
+++ b/solution.py
@@ -111,8 +111,6 @@
     near = [y * PLANE + lax.rem(xq + k, XS) * CORES + core for k in range(1, XS)] + b_to[1:] + [partner]
     for d in near:
         pl.semaphore_signal(barrier, inc=1, device_id={"dp": d}, device_id_type=MESH)
-    gpad[...] = jnp.zeros_like(gpad)
-    lp.start()
     pl.semaphore_wait(barrier, 7 + 3 + 3 + 1)
 
     def settle(ref, sem):
@@ -308,6 +306,8 @@
     for c in lw:
         c.wait()
     w_step(0)
+    gpad[...] = jnp.zeros_like(gpad)
+    lp.start()
     xa[mine, slot_cols(0)] = x_ref[own, :]
     for i in range(n):
         rows = pl.ds(pl.multiple_of(lax.rem(me + SLOTS[i] + n, n) * 32, 32), 32)

time: 62.3 us -> 62.3 us (level)
  no operation moved by 1% of the time
where the time goes in v7:
time: 62.3 us; the launch traced here: 62.2 us
  Pallas kernels  61.6 us (99%)
  between operations  0.64 us (1%)
    pallas_call x1, Pallas kernels, shards(): pl.pallas_call(main_kernel, out_shape=(VM((32, 4096), BF16), VM((8, 4096)...  59.1 us
    pallas_call x1, Pallas kernels, shards(): pl.pallas_call(error_kernel, out_shape=(S((512, 4096), BF16), S((32, 4096...  2.46 us

profile of v7, /device:TPU:1, one launch (start us, length us, event | category | flops | bytes accessed | tf_op | source)
XLA Modules:
  0.0 62.2 jit_solution(7565534972623007480)
XLA Ops:
  0.6 59.1 %shard_map.84 = (bf16[32,4096]{1,0:T(8,128)(2,1)S(1)}, f32[8,4096]{1,0:T(8,128)S(1)}, f32[512,4096]{1,0:T(8,128)S(1)}, f32[8,512]{1,0:T(8,128)S(1)}) custom-call(bf16[256,512]{1,0:T(8,128)(2,1)} %x_hbm.1, bf16[512,4096]{1,0:T(8,128)(2,1)} %w_hbm.1, bf16[32,4096]{1,0:T(8,128)(2,1)} %g_hbm.1, bf16[512,4096]{1,0:T(8,128)(2,1)} %bitcast.4, f32[8,4096]{1,0:T(8,128)} %bitcast.5), custom_call_target="tpu_custom_call" | custom-call | tf_op jit(solution)/shard_map/pallas_call | solution.py:499
  59.8 2.5 %shard_map.85 = (bf16[512,4096]{1,0:T(8,128)(2,1)}, bf16[32,4096]{1,0:T(8,128)(2,1)}, f32[8,4096]{1,0:T(8,128)}, f32[8,512]{1,0:T(8,128)}) custom-call(f32[512,4096]{1,0:T(8,128)S(1)} %get-tuple-element.12.m_ref, f32[8,512]{1,0:T(8,128)S(1)} %get-tuple-element.13.u_ref, f32[8,4096]{1,0:T(8,128)S(1)} %get-tuple-element.14.c_ref, ...), custom_call_target="tpu_custom_call" | custom-call | tf_op jit(solution)/shard_map/pallas_call | solution.py:543
